TPU v7x, 128 devices: a whole 4x4x4 slice. The times are simulated.
128 devices in a mesh: subj: 8 (over y, core), cov: 16 (over x, z).
Axes of the slice: x: 4, y: 4, z: 4, core: 2. Of those that a mesh axis runs over, the one named last changes fastest.
Arguments:
- design: bfloat16 [131072, 4096], P('subj', 'cov'), may hold values from -6 to 6
- coefs: bfloat16 [4096, 32], P('cov'), may hold values from -0.09375 to 0.09375
- penalty: float32 [32], replicated, may hold values from 0.02 to 0.3
- censor: float32 [131072], P('subj'), may hold values from 0.2 to 1
- codes: int32 [131072], P('subj'), may hold values from 0 to 2
- tie_first: int32 [131072], P('subj'), may hold values from 0 to 131071, as said below
- tie_last: int32 [131072], P('subj'), may hold values from 0 to 131071, as said below
Outputs:
- new_coefs: float32 [4096, 32], P('cov')
- weights: float32 [32, 131072], P(None, 'subj')
Inputs may be any that keep to these rules, and one draw needn't show every extreme that they name: `tie_first`: tie groups are runs of consecutive subjects; none crosses a multiple of 128. `tie_last`: the last index of the same runs as tie_first.
All inputs are finite; a program needn't handle non-finite values.
Results may differ from a plain program's by a relative error of at most 0.0003.
The roundings to bfloat16 on the way count: a program that leaves them out, or rounds other values in their place, can miss the bound.
Values sent between devices are 32-bit elements; how exact they have to be, the bound alone decides.
A program may use at most 64 MiB of HBM per device.

v0:
```python
import jax
import jax.numpy as jnp
from jax import lax
from jax.sharding import PartitionSpec as P

TIE_BLOCK = 128


def prefix(array, axis, combine, identity, reverse):
    length, index = (lax.axis_size(axis), lax.axis_index(axis))
    everything = lax.all_gather(array, axis)
    start = jnp.broadcast_to(jnp.asarray(identity, array.dtype), array.shape)

    def hop(k, before):
        at = length - 1 - k if reverse else k
        reached = at > index if reverse else at < index
        new = combine(before, everything[at])
        return jnp.where(reached, new, before)

    return lax.fori_loop(0, length, hop, start)


def add_pair(first_term, second_term):
    return first_term + second_term


def blocked_sums(values, upward):
    paths, length = values.shape
    width = 128
    count = length // width
    blocks = values.reshape(paths, count, width)
    rows = lax.broadcasted_iota(jnp.int32, (width, width), 0)
    cols = lax.broadcasted_iota(jnp.int32, (width, width), 1)
    brows = lax.broadcasted_iota(jnp.int32, (count, count), 0)
    bcols = lax.broadcasted_iota(jnp.int32, (count, count), 1)
    if upward:
        table = (rows <= cols).astype(jnp.float32)
        btable = (brows < bcols).astype(jnp.float32)
    else:
        table = (rows >= cols).astype(jnp.float32)
        btable = (brows > bcols).astype(jnp.float32)
    within = jnp.einsum("kbi,ij->kbj", blocks, table, precision=lax.Precision.HIGHEST)
    totals = within[:, :, -1] if upward else within[:, :, 0]
    offsets = jnp.dot(totals, btable, precision=lax.Precision.HIGHEST)
    return (within + offsets[:, :, None]).reshape(paths, length)


def pick_pair(first_values, second_values, local_index):
    paths, length = first_values.shape
    count = length // TIE_BLOCK
    starts = lax.broadcasted_iota(jnp.int32, (count, TIE_BLOCK), 0) * TIE_BLOCK
    inside = local_index.reshape(count, TIE_BLOCK) - starts
    slots = lax.broadcasted_iota(jnp.int32, (count, TIE_BLOCK, TIE_BLOCK), 2)
    table = (inside[:, :, None] == slots).astype(jnp.float32)
    stacked = jnp.stack([first_values, second_values]).reshape(2, paths, count, TIE_BLOCK)
    picked = jnp.einsum("skbj,bij->skbi", stacked, table, precision=lax.Precision.HIGHEST)
    picked = picked.reshape(2, paths, length)
    return (picked[0], picked[1])


def score_weights(eta, censor, codes, first_local, last_local):
    paths = eta.shape[0]
    nothing = jnp.zeros((paths,), jnp.float32)
    expo = jnp.exp(eta)
    comp = jnp.where(codes == 2, expo / censor, 0.0)
    comp_upto = blocked_sums(comp, True)
    comp_in = prefix(comp_upto[:, -1], "subj", add_pair, nothing, False)
    comp_before = comp_upto - comp + comp_in[:, None]
    risk_from = blocked_sums(expo, False)
    risk_in = prefix(risk_from[:, 0], "subj", add_pair, nothing, True)
    risk_from = risk_from + risk_in[:, None]
    risk_pick, comp_pick = pick_pair(risk_from, comp_before, first_local)
    risk = risk_pick + censor * comp_pick
    inv = jnp.where(codes == 1, 1.0 / risk, 0.0)
    heavy = inv * censor
    inv_upto = blocked_sums(inv, True)
    inv_in = prefix(inv_upto[:, -1], "subj", add_pair, nothing, False)
    inv_upto = inv_upto + inv_in[:, None]
    heavy_from = blocked_sums(heavy, False)
    heavy_in = prefix(heavy_from[:, 0], "subj", add_pair, nothing, True)
    heavy_after = heavy_from - heavy + heavy_in[:, None]
    early, later = pick_pair(inv_upto, heavy_after, last_local)
    return jnp.where(codes == 1, 1.0, 0.0) - expo * (
        early + jnp.where(codes == 2, later / censor, 0.0)
    )


def threshold(shifted, penalty):
    return jnp.sign(shifted) * jnp.maximum(jnp.abs(shifted) - penalty, 0.0)


def local(design, coefs, penalty, censor, codes, tie_first, tie_last):
    rows_here = design.shape[0]
    partial_eta = jnp.einsum("np,pk->kn", design, coefs, preferred_element_type=jnp.float32)
    eta = lax.psum(partial_eta, "cov")
    offset = lax.axis_index("subj") * rows_here
    weights = score_weights(eta, censor, codes, tie_first - offset, tie_last - offset)
    partial_score = jnp.einsum(
        "kn,np->pk", weights.astype(jnp.bfloat16), design, preferred_element_type=jnp.float32
    )
    scale = 0.1 / jnp.sqrt(jnp.float32(lax.axis_size("subj") * rows_here))
    score = lax.psum(partial_score, "subj")
    new_coefs = threshold(coefs.astype(jnp.float32) + scale * score, penalty)
    return (new_coefs, weights)


def solution(mesh):
    in_specs = (P("subj", "cov"), P("cov", None), P(), P("subj"), P("subj"), P("subj"), P("subj"))
    out_specs = (P("cov", None), P(None, "subj"))
    return jax.shard_map(local, mesh=mesh, in_specs=in_specs, out_specs=out_specs, check_vma=False)
```

profile of v0, /device:TPU:1, one launch (start us, length us, event | category | flops | bytes accessed | tf_op | source)
XLA Modules:
  0.0 263.3 jit_solution(14466235473988863869)
XLA Ops:
  7.2 7.3 %fusion.32 = f32[32,16384]{1,0:T(8,128)} fusion(bf16[256,32]{0,1:T(8,128)(2,1)} %param.16, bf16[16384,256]{1,0:T(8,128)(2,1)} %param.15), kind=kOutput, calls=%fused_computation.72 | convolution fusion | flops 268435456 | bytes 10502144 | tf_op jit(solution)/shard_map/np,pk->kn/dot_general | solution.py:94
  14.6 0.6 copy-done.13
  15.1 0.5 dynamic-slice
  16.4 90.8 %all-reduce.8.cloned.1.call-done = f32[32,16384]{1,0:T(8,128)} async-done(((f32[32,16384]{1,0:T(8,128)}), f32[32,16384]{1,0:T(8,128)}) %all-reduce.8.cloned.1.call-update) | async-done | bytes 2097168 | tf_op jit(solution)/shard_map/psum | solution.py:95
  107.2 3.3 %exponential_bitcast_fusion = (f32[4,8,128,128]{3,1,2,0:T(8,128)S(1)}, f32[4,8,128,128]{3,1,2,0:T(8,128)}) fusion(f32[32,16384]{1,0:T(8,128)} %all-reduce.8.cloned.1.call-done, f32[16384]{0:T(1024)S(1)} %copy-done.7, pred[16384]{0:T(1024)(128)(4,1)S(1)} %broadcast_compare_fusion), kind=kLoop, calls=%fused_computation.41 | loop fusion | flops 1048576 | bytes 6373376
  110.4 0.4 copy.52
  110.8 1.2 fusion.24
  112.1 0.1 fusion.21
  112.2 1.7 broadcast_add_fusion.1
  113.8 2.9 %copy.34 = f32[32,128,128]{2,1,0:T(8,128)} copy(f32[32,128,128]{1,2,0:T(8,128)} %broadcast_add_fusion.1) | data formatting | bytes 4194304 | tf_op jit(solution)/shard_map/add | solution.py:45
  116.7 3.0 %copy.72 = f32[4,8,128,128]{3,1,2,0:T(8,128)S(1)} copy(f32[4,8,128,128]{3,2,1,0:T(8,128)} %bitcast.136) | data formatting | bytes 4194304
  119.7 0.1 slice_reduce_fusion.3
  119.8 0.4 copy.54
  120.2 1.2 fusion.28
  121.4 0.1 fusion.19
  121.6 1.5 broadcast_add_fusion
  123.1 2.9 %copy.35 = f32[32,128,128]{2,1,0:T(8,128)} copy(f32[32,128,128]{1,2,0:T(8,128)} %broadcast_add_fusion) | data formatting | bytes 4194304 | tf_op jit(solution)/shard_map/add | solution.py:45
  126.1 2.8 %copy.71 = f32[4,8,128,128]{3,1,2,0:T(8,128)S(1)} copy(f32[4,8,128,128]{3,2,1,0:T(8,128)} %bitcast.133) | data formatting | bytes 4194304
  128.9 0.2 slice_reduce_fusion.2
  129.0 0.2 dynamic-update-slice
  129.3 0.2 dynamic-update-slice.1
  129.5 13.7 %all-reduce.5 = (f32[256]{0:T(256)S(1)}, f32[256]{0:T(256)S(1)}) all-reduce(f32[256]{0:T(256)S(1)} %dynamic-update-slice.1, f32[256]{0:T(256)S(1)} %dynamic-update-slice), channel_id=3, replica_groups=mesh['subj'=8,'cov'=16] {'subj'}, use_global_device_ids=true, to_apply=%add.1 | all-reduce | flops 512 | bytes 4096
  143.2 0.3 while.61
  143.5 3.7 %add_bitcast_fusion.1 = f32[4,8,128,128]{3,1,2,0:T(8,128)S(1)} fusion(f32[32]{0:T(128)S(1)} %get-tuple-element.381, f32[16384]{0:T(1024)S(1)} %copy-done.7, f32[32,16384]{1,0:T(8,128)} %all-reduce.8.cloned.1.call-done, pred[16384]{0:T(1024)(128)(4,1)S(1)} %broadcast_compare_fusion, f32[4,8,128,128]{3,2,1,0:T(8,128)} %bitcast.134), kind=kLoop, calls=%fused_computation.36 | loop fusion | flops 2097152 | bytes 6373504
  147.2 1.7 copy.56
  148.9 2.9 %copy.36 = f32[1,32,128,128]{2,3,1,0:T(8,128)} copy(f32[1,32,128,128]{3,2,1,0:T(8,128)} %bitcast.138) | data formatting | bytes 4194304 | tf_op jit(solution)/shard_map/stack | solution.py:55
  151.9 0.3 while.60
  152.3 0.3 add_bitcast_fusion.2
  152.6 1.3 copy-done.6
  153.9 2.2 pad_maximum_fusion
  156.1 5.5 %copy.37 = f32[2,32,128,128]{3,1,0,2:T(8,128)} copy(f32[2,32,128,128]{2,3,1,0:T(8,128)} %pad_maximum_fusion) | data formatting | bytes 8388608 | tf_op jit(solution)/shard_map/stack | solution.py:55
  161.5 10.7 %fusion.1 = f32[128,128,64]{1,2,0:S(1)} fusion(f32[128,128,64]{1,2,0:T(8,128)} %bitcast.132, s32[128,128]{1,0:T(8,128)S(1)} %get-tuple-element.489), kind=kOutput, calls=%fused_computation.11 | convolution fusion | flops 1612709888 | bytes 8454144
  172.3 2.6 broadcast_multiply_fusion
  174.9 3.8 %fusion.14 = f32[32,128,128]{1,2,0:T(8,128)} fusion(f32[32,128,128]{2,0,1:T(8,128)S(1)} %get-tuple-element.483), kind=kOutput, calls=%fused_computation.33 | convolution fusion | flops 805322752 | bytes 4194304 | tf_op jit(solution)/shard_map/kbi,ij->kbj/dot_general | solution.py:42
  178.6 2.4 copy.40
  181.0 0.9 slice.58
  181.9 5.2 %fusion.12 = f32[32,128,128]{1,2,0:T(8,128)} fusion(f32[32,128,128]{2,0,1:T(8,128)} %get-tuple-element.482), kind=kOutput, calls=%fused_computation.31 | convolution fusion | flops 805322752 | bytes 4194304 | tf_op jit(solution)/shard_map/kbi,ij->kbj/dot_general | solution.py:42
  187.2 3.0 %copy.44 = f32[32,128,128]{2,0,1:T(8,128)} copy(f32[32,128,128]{1,2,0:T(8,128)} %fusion.12) | data formatting | bytes 4194304 | tf_op jit(solution)/shard_map/kbi,ij->kbj/dot_general | solution.py:42
  190.2 0.9 slice.60
  191.1 0.3 fusion.18
  191.4 0.7 copy_bitcast_fusion.3
  192.1 0.2 slice_reduce_fusion.1
  192.3 0.3 fusion.20
  192.5 0.4 copy-done.2
  193.0 0.7 copy_bitcast_fusion.2
  193.7 0.1 slice_reduce_fusion
  193.8 0.2 dynamic-update-slice.2
  194.0 0.2 dynamic-update-slice.3
  194.2 13.7 %all-reduce.4 = (f32[256]{0:T(256)S(1)}, f32[256]{0:T(256)S(1)}) all-reduce(f32[256]{0:T(256)S(1)} %dynamic-update-slice.3, f32[256]{0:T(256)S(1)} %dynamic-update-slice.2), channel_id=5, replica_groups=mesh['subj'=8,'cov'=16] {'subj'}, use_global_device_ids=true, to_apply=%add.3 | all-reduce | flops 512 | bytes 4096
  208.1 0.3 while.62
  208.4 1.8 add_bitcast_fusion
  210.3 0.3 while.63
  210.6 3.5 %fusion.8 = f32[1,32,128,128]{3,1,0,2:T(8,128)S(1)} fusion(f32[2,32,128,128]{3,1,0,2:T(8,128)} %bitcast.129, f32[32,128,128]{2,0,1:T(8,128)} %copy.44, f32[32]{0:T(128)S(1)} %get-tuple-element.383, f32[128,128]{1,0:T(8,128)S(1)} %bitcast.144, f32[32,128]{0,1:T(8,128)S(1)} %fusion.20, pred[128,128]{1,0:T(8,128)(4,1)S(1)} %bitcast.146), kind=kLoop, calls=%fused_computation.26 | loop fusion | flops 4194304 | bytes 8487040 | tf_op jit(solution)/shard_map/add | solution.py:81
  214.1 0.6 pad_maximum_fusion.1
  214.7 11.2 %fusion = f32[128,128,64]{1,2,0:S(1)} fusion(f32[128,128,64]{1,2,0:T(8,128)S(1)} %bitcast.130, s32[128,128]{1,0:T(8,128)S(1)} %get-tuple-element.488), kind=kOutput, calls=%fused_computation.10 | convolution fusion | flops 1612709888 | bytes 8454144
  225.9 0.5 fusion.31
  226.4 1.2 copy.46
  227.6 1.2 copy.47
  228.9 0.4 copy-done.1
  229.3 2.9 %fusion.7 = f32[32,16384]{1,0:T(8,128)S(1)} fusion(f32[4,8,128,128]{3,2,1,0:T(8,128)S(1)} %bitcast.140, f32[4,8,128,128]{3,2,1,0:T(8,128)S(1)} %bitcast.139, f32[32,16384]{1,0:T(8,128)S(1)} %copy-done.1, f32[16384]{0:T(1024)S(1)} %copy-done.7, f32[16384]{0:T(1024)S(1)} %get-tuple-element.480, pred[16384]{0:T(1024)(128)(4,1)S(1)} %broadcast_compare_fusion), kind=kLoop, calls=%fused_computation.20 | loop fusion | flops 2621440 | bytes 8536064 | tf_op jit(solution)/shard_map/sub | solution.py:83
  232.2 1.3 copy-done.4
  233.5 1.5 convolution_bitcast_fusion
  235.1 20.7 %psum.15 = f32[256,32]{0,1:T(8,128)S(1)} all-reduce(f32[256,32]{0,1:T(8,128)S(1)} %convolution_bitcast_fusion), channel_id=1, replica_groups=mesh['subj'=8,'cov'=16] {'subj'}, use_global_device_ids=true, to_apply=%region_9.10 | all-reduce | flops 8192 | bytes 65536 | tf_op jit(solution)/shard_map/psum | solution.py:102
  255.8 0.7 maximum_multiply_fusion
  (80 shorter events, 1.1 us)
Async XLA Ops:
  7.2 100.0 %all-reduce.8.cloned.1.call-start = ((), (), s32[]{:S(2)}) async-start(), calls=%async_computation | async-start | bytes 4194304 | tf_op jit(solution)/shard_map/psum | solution.py:95
  14.5 0.7 copy-start.13
  14.5 1.8 copy-start.9
  14.5 1.8 copy-start.10
  14.5 1.9 copy-start.8
  14.5 92.7 %copy-start.7 = (f32[16384]{0:T(1024)S(1)}, f32[16384]{0:T(1024)}, u32[]{:S(2)}) copy-start(f32[16384]{0:T(1024)} %param.18) | copy-start | bytes 196612
  116.7 3.1 %copy-start.3 = (f32[4,8,128,128]{3,1,2,0:T(8,128)S(1)}, f32[4,8,128,128]{3,1,2,0:T(8,128)}, u32[]{:S(2)}) copy-start(f32[4,8,128,128]{3,1,2,0:T(8,128)} %get-tuple-element.487) | copy-start | bytes 6291460
  152.3 1.6 copy-start.6
  172.3 2.6 copy-start
  191.4 1.6 copy-start.2
  210.6 3.5 %copy-start.5 = (f32[1,32,128,128]{3,1,0,2:T(8,128)S(1)}, f32[1,32,128,128]{3,1,0,2:T(8,128)}, u32[]{:S(2)}) copy-start(f32[1,32,128,128]{3,1,0,2:T(8,128)} %add_bitcast_fusion) | copy-start | bytes 6291460
  226.4 7.1 %slice-start = ((s8[8388608]{0:T(1024)(128)(4,1)}), s8[4194304]{0:T(1024)(128)(4,1)S(1)}, s32[]{:S(2)}) async-start(s8[8388608]{0:T(1024)(128)(4,1)} %bitcast.126), calls=%async_computation.1 | async-start | bytes 8388608
  227.6 1.6 copy-start.1
  229.3 4.3 %slice-start.1 = ((s8[8388608]{0:T(1024)(128)(4,1)}), s8[4194304]{0:T(1024)(128)(4,1)S(1)}, s32[]{:S(2)}) async-start(s8[8388608]{0:T(1024)(128)(4,1)} %bitcast.126), calls=%async_computation.2 | async-start | bytes 8388608
  232.2 1.3 copy-start.4
  233.5 22.3 %copy-start.11 = (bf16[256,32]{0,1:T(8,128)(2,1)S(1)}, bf16[256,32]{0,1:T(8,128)(2,1)}, u32[]{:S(2)}) copy-start(bf16[256,32]{0,1:T(8,128)(2,1)} %param.16) | copy-start | bytes 49156
  233.5 22.3 %copy-start.12 = (f32[32]{0:T(128)S(1)}, f32[32]{0:T(128)}, u32[]{:S(2)}) copy-start(f32[32]{0:T(128)} %param.17) | copy-start | bytes 388
Sparse Core Ops, SparseCore 0:
  14.6 92.4 all-reduce.7
where the time goes:
time: 266 us; the launch traced here: 263 us
  waiting for transfers between devices  90.8 us (34%)
  blocking collectives  48.1 us (18%)
  matrix products  42.9 us (16%)
  local copies, waits for them, and re-layouts  39.1 us (15%)
  other arithmetic  26.7 us (10%)
  between operations  15 us (6%)
    psum x1, waiting for transfers between devices, local(): eta = lax.psum(partial_eta, 'cov')  90.8 us
    unnamed x2, blocking collectives  27.4 us
    unnamed x2, matrix products  21.9 us
    psum x1, blocking collectives, local(): score = lax.psum(partial_score, 'subj')  20.7 us
    unnamed x46, local copies, waits for them, and re-layouts  13.7 us
    dot_general x4, matrix products, blocked_sums(): jnp.einsum('kbi,ij->kbj', blocks, table, precision=lax.Precision.HIGHEST)  11.4 us
    another operation x2, local copies, waits for them, and re-layouts, pick_pair(): jnp.stack([first_values, second_values]).reshape(2, paths, count, TIE_BLOCK)  8.43 us
    dot_general x1, matrix products, local(): jnp.einsum('np,pk->kn', design, coefs, preferred_element_type=jnp.float32)  7.26 us
  transfers between devices with their start and end apart: 1, of which 1 were waited for; matrix products, arithmetic and copies ran while one was open for 0% of the time, Pallas kernels for 0%

commit v1 on v0

v1 whole, which is shorter than its diff:
```python
import functools

import jax
import jax.numpy as jnp
from jax import lax
from jax.experimental import pallas as pl
from jax.experimental.pallas import tpu as pltpu
from jax.sharding import PartitionSpec as P

MESH = pl.DeviceIdType.MESH
F32 = jnp.float32
BF16 = jnp.bfloat16
LANES = 128
SUBJ = 8
RING = 4
PATHS = 32
ROWS = 16384
COLS = 256
BLOCKS = ROWS // LANES
HALF = BLOCKS // 2
QUART = BLOCKS // 4
CHUNK = ROWS // 4
TILE = 1024
NBATCH = 2
COPIES = 128


def split3(x):
    high = x.astype(BF16)
    rest = x - high.astype(F32)
    mid = rest.astype(BF16)
    low = (rest - mid.astype(F32)).astype(BF16)
    return high, mid, low


def dot(a, b):
    return jnp.dot(a, b, preferred_element_type=F32)


def table(kind, wide):
    shape = (LANES, 2 * LANES if wide else LANES)
    row = lax.broadcasted_iota(jnp.int32, shape, 0)
    col = lax.broadcasted_iota(jnp.int32, shape, 1)
    keep = {"ge": row >= col, "lt": row < col, "le": row <= col, "gt": row > col}[kind]
    if wide:
        keep = keep | (col >= LANES)
    return jnp.where(keep, 1.0, 0.0).astype(BF16)


def lane_scan(x, kind):
    wide = table(kind, True)
    high, mid, low = split3(x)
    both = dot(high, wide) + (dot(mid, wide) + dot(low, wide))
    return both[:, :LANES], both[:, LANES:]


def row_scan(totals, kind):
    side = table(kind, False)
    high, mid, low = split3(totals)
    return dot(side, high) + (dot(side, mid) + dot(side, low))


def pick(values, lanes):
    return jnp.take_along_axis(values, lanes, axis=1)


def fold(x):
    return x.reshape(BLOCKS // 8, 8, LANES).sum(axis=0)


def kernel(
    design, coefs, penalty, censor, codes, first, last,
    new_out, weights_out,
    D, C, PEN, CEN, COD, FST, LST, IC2, CT, E, R1, R2, S, R3, R4, ETA, EX, BASE, TS, TR, W, OUTV, SP, SR,
    load_sem, out_sem, send_sem, recv_sem,
):
    s = lax.axis_index("subj")
    cov = lax.axis_index("cov")
    x = cov // RING
    z = cov % RING
    pos = (x, z)

    E5 = E.reshape(RING, RING, 2, BLOCKS, LANES)
    W5 = W.reshape(RING, RING, 2, BLOCKS, LANES)

    def device(axis, at):
        return (s, at * RING + z) if axis == 0 else (s, x * RING + at)

    def ring(axis):
        me = pos[axis]
        return (me + 3) % RING, (me + 1) % RING, (me + 2) % RING

    count = [0]
    started = []

    def send(src, dst, to):
        at = count[0]
        count[0] += 1
        copy = pltpu.make_async_remote_copy(
            src_ref=src, dst_ref=dst, send_sem=send_sem.at[at], recv_sem=recv_sem.at[at],
            device_id=to, device_id_type=MESH,
        )
        copy.start()
        started.append(copy)
        return copy

    loads = []
    for i, (src, dst) in enumerate(
        [(coefs, C), (penalty, PEN), (censor, CEN), (codes, COD), (first, FST), (last, LST)]
    ):
        loads.append(pltpu.make_async_copy(src, dst, load_sem.at[4 + i]))
    order = (0, 2, 1, 3)
    chunks = {}
    for i in order:
        part = pl.ds(i * CHUNK, CHUNK)
        chunks[i] = pltpu.make_async_copy(design.at[part], D.at[part], load_sem.at[i])
    loads[0].start()
    for i in order:
        chunks[i].start()
    for copy in loads[1:]:
        copy.start()

    barrier = pltpu.get_barrier_semaphore()
    peers = [device(axis, at) for axis in (0, 1) for at in ring(axis)[:2]]
    peers += [((s + d) % SUBJ, cov) for d in range(1, SUBJ)]
    for peer in peers:
        pl.semaphore_signal(barrier, inc=1, device_id=peer, device_id_type=MESH)

    loads[0].wait()
    eye = (
        lax.broadcasted_iota(jnp.int32, (PATHS, PATHS), 0)
        == lax.broadcasted_iota(jnp.int32, (PATHS, PATHS), 1)
    )
    nt = (((1,), (1,)), ((), ()))
    CT[...] = lax.dot_general(
        jnp.where(eye, 1.0, 0.0).astype(BF16), C[...], nt, preferred_element_type=F32
    )
    lhs = CT[...].astype(BF16)

    def predict(chunk):
        def body(i, carry):
            start = pl.multiple_of(chunk * CHUNK + i * TILE, TILE)
            part = lax.dot_general(lhs, D[pl.ds(start, TILE), :], nt, preferred_element_type=F32)
            for j in range(TILE // LANES):
                block = chunk * QUART + i * (TILE // LANES) + j
                for g in range(4):
                    E[pl.ds(g * 8 * BLOCKS + block, 8, stride=BLOCKS), :] = part[
                        g * 8 : g * 8 + 8, j * LANES : (j + 1) * LANES
                    ]
            return carry

        lax.fori_loop(0, CHUNK // TILE, body, 0)

    def quarter(ref, half, at, k, start, size):
        rows = pl.ds(half * HALF + start, size)
        return ref.at[at, :, k, rows, :] if half == 0 else ref.at[:, at, k, rows, :]

    sent = {}

    def rs_a(h, k, part):
        left, right, opposite = ring(h)
        start = part * QUART
        near, far = ((left, right) if part == 0 else (right, left))
        d_far, d_near = (0, 1) if part == 0 else (1, 0)
        sent["m1", h, k, d_far] = send(
            quarter(E5, h, opposite, k, start, QUART), R1.at[h, k, d_far], device(h, far)
        )
        sent["m2", h, k, d_near] = send(
            quarter(E5, h, near, k, start, QUART),
            R2.at[h, k, d_near, :, pl.ds(start, QUART), :],
            device(h, near),
        )

    def rs_b(h, k):
        left, right, opposite = ring(h)
        for d, to, start in ((0, right, 0), (1, left, QUART)):
            sent["m1", h, k, d].wait_recv()
            mine = quarter(E5, h, to, k, start, QUART)
            mine[...] = mine[...] + R1[h, k, d]
            sent["m3", h, k, d] = send(
                mine, R2.at[h, k, d, :, pl.ds(start, QUART), :], device(h, to)
            )

    def rs_c(h, k):
        for d in (0, 1):
            sent["m2", h, k, d].wait_recv()
            sent["m3", h, k, d].wait_recv()
        S[h, k] = quarter(E5, h, pos[h], k, 0, HALF)[...] + R2[h, k, 0] + R2[h, k, 1]
        g = 1 - h
        left, right, opposite = ring(g)
        lo, hi = pl.ds(0, QUART), pl.ds(QUART, QUART)
        sent["n1", h, k, 0] = send(S.at[h, k, opposite, lo, :], R3.at[h, k, 0], device(g, right))
        sent["n1", h, k, 1] = send(S.at[h, k, opposite, hi, :], R3.at[h, k, 1], device(g, left))
        sent["n2", h, k, 1] = send(S.at[h, k, left, lo, :], R4.at[h, k, 1, lo, :], device(g, left))
        sent["n2", h, k, 0] = send(S.at[h, k, right, hi, :], R4.at[h, k, 0, hi, :], device(g, right))

    def rs_d(h, k):
        g = 1 - h
        left, right, opposite = ring(g)
        for d, to, start in ((0, right, 0), (1, left, QUART)):
            sent["n1", h, k, d].wait_recv()
            mine = S.at[h, k, to, pl.ds(start, QUART), :]
            mine[...] = mine[...] + R3[h, k, d]
            sent["n3", h, k, d] = send(
                mine, R4.at[h, k, d, pl.ds(start, QUART), :], device(g, to)
            )

    def rs_e(h, k):
        for d in (0, 1):
            sent["n2", h, k, d].wait_recv()
            sent["n3", h, k, d].wait_recv()
        ETA[k, pl.ds(h * HALF, HALF), :] = S[h, k, pos[1 - h]] + R4[h, k, 0] + R4[h, k, 1]

    def exchange(k, e):
        for d in range(1, SUBJ):
            sent["t", k, e, d] = send(TS.at[k, e], TR.at[k, e, d], ((s + d) % SUBJ, cov))

    def arrived(k, e):
        after = jnp.zeros((8, LANES), F32)
        before = jnp.zeros((8, LANES), F32)
        for d in range(1, SUBJ):
            sent["t", k, e, d].wait_recv()
            after = after + jnp.where(d > s, TR[k, e, d, 0], 0.0)
            before = before + jnp.where(d <= s, TR[k, e, d, 1], 0.0)
        return jnp.sum(after, keepdims=True), jnp.sum(before, keepdims=True)

    def prepare():
        for copy in loads[1:]:
            copy.wait()
        FST[...] = FST[...] & (LANES - 1)
        LST[...] = LST[...] & (LANES - 1)
        IC2[...] = jnp.where(COD[...] == 2, 1.0 / CEN[...], 0.0)

    def scan_a(k):
        expo = jnp.exp(ETA[k])
        comp = expo * IC2[...]
        EX[k] = expo
        TS[k, 0, 0] = fold(expo)
        TS[k, 0, 1] = fold(comp)
        exchange(k, 0)
        risk, risk_rows = lane_scan(expo, "ge")
        before, before_rows = lane_scan(comp, "lt")
        lanes = FST[...]
        BASE[k] = (pick(risk, lanes) + row_scan(risk_rows, "lt")) + CEN[...] * (
            pick(before, lanes) + row_scan(before_rows, "gt")
        )

    def scan_b(k):
        risk_in, comp_in = arrived(k, 0)
        risk = BASE[k] + (risk_in + CEN[...] * comp_in)
        inv = jnp.where(COD[...] == 1, 1.0 / risk, 0.0)
        heavy = inv * CEN[...]
        TS[k, 1, 0] = fold(heavy)
        TS[k, 1, 1] = fold(inv)
        exchange(k, 1)
        upto, upto_rows = lane_scan(inv, "le")
        later, later_rows = lane_scan(heavy, "gt")
        lanes = LST[...]
        BASE[k] = (pick(upto, lanes) + row_scan(upto_rows, "gt")) + IC2[...] * (
            pick(later, lanes) + row_scan(later_rows, "lt")
        )

    def scan_c(k):
        later_in, early_in = arrived(k, 1)
        event = jnp.where(COD[...] == 1, 1.0, 0.0)
        W5[x, z, k] = event - EX[k] * (BASE[k] + (early_in + IC2[...] * later_in))

    def spot(h, k, axis, at, start, size):
        rows = pl.ds(h * HALF + start, size)
        if axis == 0:
            return W5.at[at, z, k, rows, :]
        return W5.at[x, at, k, rows, :]

    def ag_a(h, k):
        g = 1 - h
        left, right, opposite = ring(g)
        mine = spot(h, k, g, pos[g], 0, HALF)
        sent["a1", h, k, 0] = send(mine, mine, device(g, right))
        sent["a1", h, k, 1] = send(mine, mine, device(g, left))

    def ag_b(h, k):
        g = 1 - h
        left, right, opposite = ring(g)
        for d, came, to, start in ((0, left, right, 0), (1, right, left, QUART)):
            sent["a1", h, k, d].wait_recv()
            piece = spot(h, k, g, came, start, QUART)
            sent["a2", h, k, d] = send(piece, piece, device(g, to))

    def ag_c(h, k):
        left, right, opposite = ring(h)
        for d in (0, 1):
            sent["a2", h, k, d].wait_recv()
        mine = quarter(W5, h, pos[h], k, 0, HALF)
        sent["a3", h, k, 0] = send(mine, mine, device(h, right))
        sent["a3", h, k, 1] = send(mine, mine, device(h, left))

    def ag_d(h, k):
        left, right, opposite = ring(h)
        for d, came, to, start in ((0, left, right, 0), (1, right, left, QUART)):
            sent["a3", h, k, d].wait_recv()
            piece = quarter(W5, h, came, k, start, QUART)
            sent["a4", h, k, d] = send(piece, piece, device(h, to))

    def ag_e(h, k):
        for d in (0, 1):
            sent["a4", h, k, d].wait_recv()

    for i, (chunk, h, part) in enumerate(((0, 0, 0), (2, 1, 0), (1, 0, 1), (3, 1, 1))):
        chunks[chunk].wait()
        predict(chunk)
        if i == 0:
            pl.semaphore_wait(barrier, len(peers))
        rs_a(h, 0, part)
    both = (0, 1)
    for h in both:
        rs_b(h, 0)
    for h in both:
        rs_a(h, 1, 0)
        rs_a(h, 1, 1)
    prepare()
    for h in both:
        rs_c(h, 0)
    for h in both:
        rs_d(h, 0)
    for h in both:
        rs_b(h, 1)
    for h in both:
        rs_e(h, 0)
    scan_a(0)
    for h in both:
        rs_c(h, 1)
    scan_b(0)
    for h in both:
        rs_d(h, 1)
    for h in both:
        rs_e(h, 1)
    scan_a(1)
    scan_c(0)
    for h in both:
        ag_a(h, 0)
    scan_b(1)
    for h in both:
        ag_b(h, 0)
    for h in both:
        ag_c(h, 0)
    scan_c(1)
    for h in both:
        ag_a(h, 1)
    for h in both:
        ag_b(h, 1)
    for h in both:
        ag_d(h, 0)
    for h in both:
        ag_c(h, 1)
    for h in both:
        ag_e(h, 0)
    for h in both:
        ag_d(h, 1)
    for h in both:
        ag_e(h, 1)

    def accumulate(i, total):
        start = pl.multiple_of(i * TILE, TILE)
        parts = []
        for j in range(TILE // LANES):
            block = i * (TILE // LANES) + j
            parts.append(
                jnp.concatenate(
                    [W[pl.ds(g * 8 * BLOCKS + block, 8, stride=BLOCKS), :] for g in range(4)], axis=0
                )
            )
        tile = jnp.concatenate(parts, axis=1)
        OUTV[:, pl.ds(start, TILE)] = tile
        return total + dot(tile.astype(BF16), D[pl.ds(start, TILE), :])

    total = jnp.zeros((PATHS, COLS), F32)
    outs = []
    for c in range(4):
        total = lax.fori_loop(c * (CHUNK // TILE), (c + 1) * (CHUNK // TILE), accumulate, total)
        part = pl.ds(c * CHUNK, CHUNK)
        copy = pltpu.make_async_copy(OUTV.at[:, part], weights_out.at[:, part], out_sem.at[c])
        copy.start()
        outs.append(copy)
    SP[...] = total
    for d in range(1, SUBJ):
        sent["s", d] = send(SP, SR.at[s], ((s + d) % SUBJ, cov))
    SR[s] = total
    for d in range(1, SUBJ):
        sent["s", d].wait_recv()
    score = SR[0]
    for i in range(1, SUBJ):
        score = score + SR[i]
    scale = 0.1 / jnp.sqrt(F32(SUBJ * ROWS))
    limit = jnp.sum(jnp.where(eye, jnp.broadcast_to(PEN[...], (PATHS, PATHS)), 0.0), axis=1, keepdims=True)
    shifted = CT[...] + scale * score
    sign = jnp.where(shifted > 0, 1.0, jnp.where(shifted < 0, -1.0, 0.0))
    new_out[...] = sign * jnp.maximum(jnp.abs(shifted) - limit, 0.0)
    for copy in outs:
        copy.wait()
    for copy in started:
        copy.wait_send()


def local(design, coefs, penalty, censor, codes, tie_first, tie_last):
    square = (BLOCKS, LANES)
    anywhere = pl.BlockSpec(memory_space=pl.ANY)
    vmem = pltpu.VMEM
    dma = pltpu.SemaphoreType.DMA
    new, weights = pl.pallas_call(
        kernel,
        out_shape=(
            jax.ShapeDtypeStruct((PATHS, COLS), F32),
            jax.ShapeDtypeStruct((PATHS, ROWS), F32),
        ),
        in_specs=[anywhere] * 7,
        out_specs=(pl.BlockSpec(memory_space=pltpu.VMEM), anywhere),
        scratch_shapes=[
            vmem((ROWS, COLS), BF16),
            vmem((COLS, PATHS), BF16),
            vmem((1, PATHS), F32),
            vmem(square, F32),
            vmem(square, jnp.int32),
            vmem(square, jnp.int32),
            vmem(square, jnp.int32),
            vmem(square, F32),
            vmem((PATHS, COLS), F32),
            vmem((PATHS * BLOCKS, LANES), F32),
            vmem((2, NBATCH, 2, RING, QUART, LANES), F32),
            vmem((2, NBATCH, 2, RING, HALF, LANES), F32),
            vmem((2, NBATCH, RING, HALF, LANES), F32),
            vmem((2, NBATCH, 2, QUART, LANES), F32),
            vmem((2, NBATCH, 2, HALF, LANES), F32),
            vmem((NBATCH, BLOCKS, LANES), F32),
            vmem((NBATCH, BLOCKS, LANES), F32),
            vmem((NBATCH, BLOCKS, LANES), F32),
            vmem((NBATCH, 2, 2, 8, LANES), F32),
            vmem((NBATCH, 2, SUBJ, 2, 8, LANES), F32),
            vmem((PATHS * BLOCKS, LANES), F32),
            vmem((PATHS, ROWS), F32),
            vmem((PATHS, COLS), F32),
            vmem((SUBJ, PATHS, COLS), F32),
            dma((10,)),
            dma((4,)),
            dma((COPIES,)),
            dma((COPIES,)),
        ],
        compiler_params=pltpu.CompilerParams(
            collective_id=0, has_side_effects=True, vmem_limit_bytes=48 * 2**20
        ),
        cost_estimate=pl.CostEstimate(
            flops=4 * PATHS * ROWS * COLS,
            bytes_accessed=2 * ROWS * COLS + 4 * PATHS * ROWS,
            transcendentals=2 * ROWS,
        ),
    )(
        design,
        coefs,
        penalty.reshape(1, PATHS),
        censor.reshape(square),
        codes.reshape(square),
        tie_first.reshape(square),
        tie_last.reshape(square),
    )
    return new.T, weights


def solution(mesh):
    in_specs = (P("subj", "cov"), P("cov", None), P(), P("subj"), P("subj"), P("subj"), P("subj"))
    out_specs = (P("cov", None), P(None, "subj"))
    return jax.shard_map(local, mesh=mesh, in_specs=in_specs, out_specs=out_specs, check_vma=False)
```

time: 266 us -> 77.8 us (0.29)
  waiting for transfers between devices: 90.8 us -> 0 us
  Pallas kernels: 0 us -> 70 us
  blocking collectives: 48.1 us -> 0 us
  matrix products: 42.9 us -> 0 us
  local copies, waits for them, and re-layouts: 39.1 us -> 6.78 us
  other arithmetic: 26.7 us -> 0 us
  between operations: 15 us -> 0.65 us
    psum x1 -> x0, waiting for transfers between devices: 90.8 us -> none  [local(): eta = lax.psum(partial_eta, 'cov')]
    pallas_call x0 -> x1, Pallas kernels: none -> 70 us  [local(): pl.pallas_call(kernel, out_shape=(jax.ShapeDtypeStruct((PATHS, COLS), F32...]
    unnamed x2 -> x0, blocking collectives: 27.4 us -> none
    unnamed x2 -> x0, matrix products: 21.9 us -> none
    dot_general x10 -> x0, matrix products: 21 us -> none  [the longest x4 11.4 us: blocked_sums(): jnp.einsum('kbi,ij->kbj', blocks, table, precision=lax.Precision.HIGHEST)]
    psum x1 -> x0, blocking collectives: 20.7 us -> none  [local(): score = lax.psum(partial_score, 'subj')]
    add x5 -> x0, other arithmetic: 8.8 us -> none  [the longest x1 3.47 us: score_weights(): heavy_after = heavy_from - heavy + heavy_in[:, None]]
    another operation x2 -> x0, local copies, waits for them, and re-layouts: 8.43 us -> none  [pick_pair(): jnp.stack([first_values, second_values]).reshape(2, paths, count, TIE_BLOCK)]
  transfers between devices with their start and end apart: 1 -> 0, of which waited for: 1 -> 0; matrix products, arithmetic and copies ran while one was open for 0% -> 0% of each run, Pallas kernels for 0% -> 0%
where the time goes in v1:
time: 77.8 us; the launch traced here: 77.4 us
  Pallas kernels  70 us (90%)
  local copies, waits for them, and re-layouts  6.78 us (9%)
    pallas_call x1, Pallas kernels, local(): pl.pallas_call(kernel, out_shape=(jax.ShapeDtypeStruct((PATHS, COLS), F32...  70 us
    unnamed x13, local copies, waits for them, and re-layouts  6.78 us

profile of v1, /device:TPU:1, one launch (start us, length us, event | category | flops | bytes accessed | tf_op | source)
XLA Modules:
  0.0 77.4 jit_solution(205573409613504375)
XLA Ops:
  0.6 0.8 %copy.9.coefs = bf16[256,32]{1,0:T(8,128)(2,1)S(1)} copy(bf16[256,32]{0,1:T(8,128)(2,1)} %param.8) | data formatting | bytes 32768 | tf_op args[1]
  1.5 0.0 copy-start
  1.5 0.8 %copy-done = f32[16384]{0:T(1024)S(1)} copy-done((f32[16384]{0:T(1024)S(1)}, f32[16384]{0:T(1024)}, u32[]{:S(2)}) %copy-start) | copy-done | bytes 65560
  2.3 0.0 copy-start.1
  2.3 0.8 %copy-done.1 = s32[16384]{0:T(1024)S(1)} copy-done((s32[16384]{0:T(1024)S(1)}, s32[16384]{0:T(1024)}, u32[]{:S(2)}) %copy-start.1) | copy-done | bytes 65560
  3.1 0.0 copy-start.2
  3.2 0.8 %copy-done.2 = s32[16384]{0:T(1024)S(1)} copy-done((s32[16384]{0:T(1024)S(1)}, s32[16384]{0:T(1024)}, u32[]{:S(2)}) %copy-start.2) | copy-done | bytes 65560
  4.0 0.0 copy-start.3
  4.0 0.8 %copy-done.3 = s32[16384]{0:T(1024)S(1)} copy-done((s32[16384]{0:T(1024)S(1)}, s32[16384]{0:T(1024)}, u32[]{:S(2)}) %copy-start.3) | copy-done | bytes 65560
  4.8 0.0 copy-start.4
  4.8 0.7 copy-done.4
  5.5 70.0 %shard_map.86 = (f32[32,256]{1,0:T(8,128)S(1)}, f32[32,16384]{1,0:T(8,128)S(1)}) custom-call(bf16[16384,256]{1,0:T(8,128)(2,1)} %design.1, bf16[256,32]{1,0:T(8,128)(2,1)S(1)} %copy.9.coefs, f32[1,32]{1,0:T(1,128)S(1)} %bitcast.11, f32[128,128]{1,0:T(8,128)S(1)} %bitcast.6, s32[128,128]{1,0:T(8,128)S(1)} %bitcast.7, s32[128,128]{1,0:T(8,128)S(1)} %bitcast.8, ...), custom_call_target="tpu_custom_call" | custom-call | flops 536870912 | bytes 10485760 | tf_op jit(solution)/shard_map/pallas_call | solution.py:409
  75.5 0.6 copy.12
  76.1 1.3 %copy.13 = f32[32,16384]{1,0:T(8,128)} copy(f32[32,16384]{1,0:T(8,128)S(1)} %get-tuple-element.9) | data formatting | bytes 4194304
Async XLA Ops:
  1.5 0.8 %copy-start = (f32[16384]{0:T(1024)S(1)}, f32[16384]{0:T(1024)}, u32[]{:S(2)}) copy-start(f32[16384]{0:T(1024)} %param.10) | copy-start | bytes 196612
  2.3 0.8 %copy-start.1 = (s32[16384]{0:T(1024)S(1)}, s32[16384]{0:T(1024)}, u32[]{:S(2)}) copy-start(s32[16384]{0:T(1024)} %param.11) | copy-start | bytes 196612
  3.1 0.8 %copy-start.2 = (s32[16384]{0:T(1024)S(1)}, s32[16384]{0:T(1024)}, u32[]{:S(2)}) copy-start(s32[16384]{0:T(1024)} %param.12) | copy-start | bytes 196612
  4.0 0.8 %copy-start.3 = (s32[16384]{0:T(1024)S(1)}, s32[16384]{0:T(1024)}, u32[]{:S(2)}) copy-start(s32[16384]{0:T(1024)} %param.13) | copy-start | bytes 196612
  4.8 0.7 copy-start.4

commit v2 on v1

v2 whole, which is shorter than its diff:
```python
import functools

import jax
import jax.numpy as jnp
from jax import lax
from jax.experimental import pallas as pl
from jax.experimental.pallas import tpu as pltpu
from jax.sharding import PartitionSpec as P

MESH = pl.DeviceIdType.MESH
F32 = jnp.float32
BF16 = jnp.bfloat16
LANES = 128
SUBJ = 8
RING = 4
PATHS = 32
ROWS = 16384
COLS = 256
BLOCKS = ROWS // LANES
HALF = BLOCKS // 2
QUART = BLOCKS // 4
CHUNK = ROWS // 4
TILE1 = 4096
TILE2 = 4096
NBATCH = 2


def split3(x):
    high = x.astype(BF16)
    rest = x - high.astype(F32)
    mid = rest.astype(BF16)
    low = (rest - mid.astype(F32)).astype(BF16)
    return high, mid, low


def dot(a, b):
    return jnp.dot(a, b, preferred_element_type=F32)


def table(kind, wide):
    shape = (LANES, 2 * LANES if wide else LANES)
    row = lax.broadcasted_iota(jnp.int32, shape, 0)
    col = lax.broadcasted_iota(jnp.int32, shape, 1)
    keep = {"ge": row >= col, "lt": row < col, "le": row <= col, "gt": row > col}[kind]
    if wide:
        keep = keep | (col >= LANES)
    return jnp.where(keep, 1.0, 0.0).astype(BF16)


def lane_scan(x, kind):
    wide = table(kind, True)
    high, mid, low = split3(x)
    both = dot(high, wide) + (dot(mid, wide) + dot(low, wide))
    return both[:, :LANES], both[:, LANES:]


def row_scan(totals, kind):
    side = table(kind, False)
    high, mid, low = split3(totals)
    return dot(side, high) + (dot(side, mid) + dot(side, low))


def pick(values, lanes):
    return jnp.take_along_axis(values, lanes, axis=1)


def fold(x):
    return x.reshape(BLOCKS // 8, 8, LANES).sum(axis=0)


def kernel(
    design, coefs, penalty, censor, codes, first, last,
    new_out, weights_out,
    D, C, PEN, CEN, COD, FST, LST, IC2, E, R1, R2, S, R4, ETA, EX, BASE, TS, TR, W, SP, SR, SUM,
    load_sem, send_sem, recv_sem,
):
    s = lax.axis_index("subj")
    cov = lax.axis_index("cov")
    x = cov // RING
    z = cov % RING
    pos = (x, z)

    E5 = E.reshape(RING, RING, 2, BLOCKS, LANES)
    W5 = W.reshape(RING, RING, 2, BLOCKS, LANES)

    def device(axis, at):
        return (s, at * RING + z) if axis == 0 else (s, x * RING + at)

    def ring(axis):
        me = pos[axis]
        return (me + 3) % RING, (me + 1) % RING, (me + 2) % RING

    sent_rows = [0]
    groups = {}

    def rows_of(ref):
        size = 1
        for n in ref.shape[:-1]:
            size *= n
        return size * ref.shape[-1] // LANES

    def send(group, src, dst, to):
        at, rows = groups.get(group, (len(groups), 0))
        groups[group] = (at, rows + rows_of(src))
        sent_rows[0] += rows_of(src)
        pltpu.make_async_remote_copy(
            src_ref=src, dst_ref=dst, send_sem=send_sem.at[0], recv_sem=recv_sem.at[at],
            device_id=to, device_id_type=MESH,
        ).start()

    def wait_rows(sem, rows):
        span = W.at[pl.ds(0, rows), :] if rows <= PATHS * BLOCKS else None
        pltpu.make_async_copy(span, span, sem).wait()

    def received(*group):
        at, rows = groups[group]
        wait_rows(recv_sem.at[at], rows)

    order = (0, 2, 1, 3)
    chunks = {}
    for i in order:
        part = pl.ds(i * CHUNK, CHUNK)
        chunks[i] = pltpu.make_async_copy(design.at[part], D.at[part], load_sem.at[i])
    small = []
    for i, (src, dst) in enumerate(
        [(coefs, C), (penalty, PEN), (censor, CEN), (codes, COD), (first, FST), (last, LST)]
    ):
        small.append(pltpu.make_async_copy(src, dst, load_sem.at[4 + i]))
    small[0].start()
    for i in order:
        chunks[i].start()
    for copy in small[1:]:
        copy.start()

    barrier = pltpu.get_barrier_semaphore()
    peers = [device(axis, at) for axis in (0, 1) for at in ring(axis)]
    peers += [((s + d) % SUBJ, cov) for d in range(1, SUBJ)]
    for peer in peers:
        pl.semaphore_signal(barrier, inc=1, device_id=peer, device_id_type=MESH)

    small[0].wait()
    nt = (((1,), (1,)), ((), ()))
    lhs = C[...]

    def predict(chunk):
        for i in range(CHUNK // TILE1):
            start = chunk * CHUNK + i * TILE1
            part = lax.dot_general(lhs, D[start : start + TILE1, :], nt, preferred_element_type=F32)
            for j in range(TILE1 // LANES):
                block = start // LANES + j
                for g in range(4):
                    E[pl.ds(g * 8 * BLOCKS + block, 8, stride=BLOCKS), :] = part[
                        g * 8 : g * 8 + 8, j * LANES : (j + 1) * LANES
                    ]

    def quarter(ref, half, at, k, start, size):
        rows = pl.ds(half * HALF + start, size)
        return ref.at[at, :, k, rows, :] if half == 0 else ref.at[:, at, k, rows, :]

    def rs_far(h, k, part):
        left, right, opposite = ring(h)
        start, d, to = ((0, 0, right), (QUART, 1, left))[part]
        send(("m1", h, k), quarter(E5, h, opposite, k, start, QUART), R1.at[h, k, d], device(h, to))

    def rs_near(h, k, part):
        left, right, opposite = ring(h)
        start, d, to = ((0, 1, left), (QUART, 0, right))[part]
        send(
            ("m2", h, k),
            quarter(E5, h, to, k, start, QUART),
            R2.at[h, k, d, :, pl.ds(start, QUART), :],
            device(h, to),
        )

    def rs_on(h, k):
        left, right, opposite = ring(h)
        received("m1", h, k)
        for d, to, start in ((0, right, 0), (1, left, QUART)):
            mine = quarter(E5, h, to, k, start, QUART)
            mine[...] = mine[...] + R1[h, k, d]
            send(("m2", h, k), mine, R2.at[h, k, d, :, pl.ds(start, QUART), :], device(h, to))

    def rs_second(h, k):
        received("m2", h, k)
        S[h, k] = quarter(E5, h, pos[h], k, 0, HALF)[...] + R2[h, k, 0] + R2[h, k, 1]
        for slot, at in enumerate(ring(1 - h)):
            send(("n", h, k), S.at[h, k, at], R4.at[h, k, slot], device(1 - h, at))

    def rs_end(h, k):
        received("n", h, k)
        ETA[k, pl.ds(h * HALF, HALF), :] = S[h, k, pos[1 - h]] + (
            R4[h, k, 0] + R4[h, k, 1] + R4[h, k, 2]
        )

    def exchange(k, e):
        for d in range(1, SUBJ):
            send(("t", k, e), TS.at[k, e], TR.at[k, e, d], ((s + d) % SUBJ, cov))

    def arrived(k, e):
        received("t", k, e)
        after = jnp.zeros((8, LANES), F32)
        before = jnp.zeros((8, LANES), F32)
        for d in range(1, SUBJ):
            after = after + jnp.where(d > s, TR[k, e, d, 0], 0.0)
            before = before + jnp.where(d <= s, TR[k, e, d, 1], 0.0)
        return jnp.sum(after, keepdims=True), jnp.sum(before, keepdims=True)

    def prepare():
        for copy in small[1:]:
            copy.wait()
        FST[...] = FST[...] & (LANES - 1)
        LST[...] = LST[...] & (LANES - 1)
        IC2[...] = jnp.where(COD[...] == 2, 1.0 / CEN[...], 0.0)

    def scan_a(k):
        expo = jnp.exp(ETA[k])
        comp = expo * IC2[...]
        EX[k] = expo
        TS[k, 0, 0] = fold(expo)
        TS[k, 0, 1] = fold(comp)
        exchange(k, 0)
        risk, risk_rows = lane_scan(expo, "ge")
        before, before_rows = lane_scan(comp, "lt")
        lanes = FST[...]
        BASE[k] = (pick(risk, lanes) + row_scan(risk_rows, "lt")) + CEN[...] * (
            pick(before, lanes) + row_scan(before_rows, "gt")
        )

    def scan_b(k):
        risk_in, comp_in = arrived(k, 0)
        risk = BASE[k] + (risk_in + CEN[...] * comp_in)
        inv = jnp.where(COD[...] == 1, 1.0 / risk, 0.0)
        heavy = inv * CEN[...]
        TS[k, 1, 0] = fold(heavy)
        TS[k, 1, 1] = fold(inv)
        exchange(k, 1)
        upto, upto_rows = lane_scan(inv, "le")
        later, later_rows = lane_scan(heavy, "gt")
        lanes = LST[...]
        BASE[k] = (pick(upto, lanes) + row_scan(upto_rows, "gt")) + IC2[...] * (
            pick(later, lanes) + row_scan(later_rows, "lt")
        )

    def scan_c(k):
        later_in, early_in = arrived(k, 1)
        event = jnp.where(COD[...] == 1, 1.0, 0.0)
        W5[x, z, k] = event - EX[k] * (BASE[k] + (early_in + IC2[...] * later_in))

    def spot(h, k, at):
        rows = pl.ds(h * HALF, HALF)
        return W5.at[x, at, k, rows, :] if h == 0 else W5.at[at, z, k, rows, :]

    def ag_first(h, k):
        mine = spot(h, k, pos[1 - h])
        for at in ring(1 - h):
            send(("a1", h, k), mine, mine, device(1 - h, at))
        for at in ring(h):
            send(("a2", h, k), mine, mine, device(h, at))

    def ag_second(h, k):
        received("a1", h, k)
        for came in ring(1 - h):
            piece = spot(h, k, came)
            for at in ring(h):
                send(("a2", h, k), piece, piece, device(h, at))

    def ag_end(h, k):
        received("a2", h, k)

    def score(k):
        total = jnp.zeros((PATHS // 2, COLS), F32)
        for i in range(ROWS // TILE2):
            start = i * TILE2
            parts = []
            for j in range(TILE2 // LANES):
                block = start // LANES + j
                rows = [
                    W[pl.ds((g * 16 + k) * BLOCKS + block, 8, stride=2 * BLOCKS), :]
                    for g in range(2)
                ]
                parts.append(jnp.concatenate(rows, axis=0).astype(BF16))
            total = total + dot(jnp.concatenate(parts, axis=1), D[start : start + TILE2, :])
        SP[k] = total
        for d in range(1, SUBJ):
            send(("s", k), SP.at[k], SR.at[k, s], ((s + d) % SUBJ, cov))
        SR[k, s] = total

    both = (0, 1)
    for i, (chunk, h, part) in enumerate(((0, 0, 0), (2, 1, 0), (1, 0, 1), (3, 1, 1))):
        chunks[chunk].wait()
        predict(chunk)
        if i == 0:
            pl.semaphore_wait(barrier, len(peers))
        rs_far(h, 0, part)
        rs_near(h, 0, part)
    for h in both:
        rs_far(h, 1, 0)
        rs_far(h, 1, 1)
    for h in both:
        rs_on(h, 0)
    for h in both:
        rs_near(h, 1, 0)
        rs_near(h, 1, 1)
    prepare()
    for h in both:
        rs_on(h, 1)
    for k in both:
        for h in both:
            rs_second(h, k)
    for h in both:
        rs_end(h, 0)
    scan_a(0)
    for h in both:
        rs_end(h, 1)
    scan_a(1)
    for k in both:
        scan_b(k)
    for k in both:
        scan_c(k)
        for h in both:
            ag_first(h, k)
    for k in both:
        for h in both:
            ag_second(h, k)
    for h in both:
        ag_end(h, 0)
    score(0)
    for h in both:
        ag_end(h, 1)
    score(1)

    for block in range(BLOCKS):
        for g in range(4):
            weights_out[g * 8 : g * 8 + 8, block * LANES : (block + 1) * LANES] = W[
                pl.ds(g * 8 * BLOCKS + block, 8, stride=BLOCKS), :
            ]
    eye = (
        lax.broadcasted_iota(jnp.int32, (PATHS, PATHS), 0)
        == lax.broadcasted_iota(jnp.int32, (PATHS, PATHS), 1)
    )
    limit = jnp.sum(
        jnp.where(eye, jnp.broadcast_to(PEN[...], (PATHS, PATHS)), 0.0), axis=1, keepdims=True
    )
    wide = C[...].astype(F32)
    for k in both:
        received("s", k)
        total = SR[k, 0]
        for i in range(1, SUBJ):
            total = total + SR[k, i]
        for c in range(2):
            SUM[c, pl.ds(k, PATHS // 2, stride=2), :] = total[:, c * LANES : (c + 1) * LANES]
    scale = 0.1 / jnp.sqrt(F32(SUBJ * ROWS))
    for c in range(2):
        cols = slice(c * LANES, (c + 1) * LANES)
        shifted = wide[:, cols] + scale * SUM[c]
        sign = jnp.where(shifted > 0, 1.0, jnp.where(shifted < 0, -1.0, 0.0))
        new_out[:, cols] = sign * jnp.maximum(jnp.abs(shifted) - limit, 0.0)
    left_rows = sent_rows[0]
    span = D.at[pl.ds(0, left_rows), :]
    pltpu.make_async_copy(span, span, send_sem.at[0]).wait()


def local(design, coefs, penalty, censor, codes, tie_first, tie_last):
    square = (BLOCKS, LANES)
    vmem = pltpu.VMEM
    dma = pltpu.SemaphoreType.DMA
    new, weights = pl.pallas_call(
        kernel,
        out_shape=(
            jax.ShapeDtypeStruct((PATHS, COLS), F32),
            jax.ShapeDtypeStruct((PATHS, ROWS), F32),
        ),
        in_specs=[pl.BlockSpec(memory_space=pltpu.HBM)] * 7,
        out_specs=(pl.BlockSpec(memory_space=pltpu.VMEM), pl.BlockSpec(memory_space=pltpu.VMEM)),
        scratch_shapes=[
            vmem((ROWS, COLS), BF16),
            vmem((PATHS, COLS), BF16),
            vmem((1, PATHS), F32),
            vmem(square, F32),
            vmem(square, jnp.int32),
            vmem(square, jnp.int32),
            vmem(square, jnp.int32),
            vmem(square, F32),
            vmem((PATHS * BLOCKS, LANES), F32),
            vmem((2, NBATCH, 2, RING, QUART, LANES), F32),
            vmem((2, NBATCH, 2, RING, HALF, LANES), F32),
            vmem((2, NBATCH, RING, HALF, LANES), F32),
            vmem((2, NBATCH, 3, HALF, LANES), F32),
            vmem((NBATCH, BLOCKS, LANES), F32),
            vmem((NBATCH, BLOCKS, LANES), F32),
            vmem((NBATCH, BLOCKS, LANES), F32),
            vmem((NBATCH, 2, 2, 8, LANES), F32),
            vmem((NBATCH, 2, SUBJ, 2, 8, LANES), F32),
            vmem((PATHS * BLOCKS, LANES), F32),
            vmem((NBATCH, PATHS // 2, COLS), F32),
            vmem((NBATCH, SUBJ, PATHS // 2, COLS), F32),
            vmem((2, PATHS, LANES), F32),
            dma((10,)),
            dma((1,)),
            dma((26,)),
        ],
        compiler_params=pltpu.CompilerParams(
            collective_id=0, has_side_effects=True, vmem_limit_bytes=48 * 2**20
        ),
        cost_estimate=pl.CostEstimate(
            flops=4 * PATHS * ROWS * COLS,
            bytes_accessed=2 * ROWS * COLS + 4 * PATHS * ROWS,
            transcendentals=2 * ROWS,
        ),
    )(
        design,
        coefs.T,
        penalty.reshape(1, PATHS),
        censor.reshape(square),
        codes.reshape(square),
        tie_first.reshape(square),
        tie_last.reshape(square),
    )
    return new.T, weights


def solution(mesh):
    in_specs = (P("subj", "cov"), P("cov", None), P(), P("subj"), P("subj"), P("subj"), P("subj"))
    out_specs = (P("cov", None), P(None, "subj"))
    return jax.shard_map(local, mesh=mesh, in_specs=in_specs, out_specs=out_specs, check_vma=False)
```

time: 77.8 us -> 61.8 us (0.79)
  Pallas kernels: 70 us -> 54.1 us
    pallas_call x1, Pallas kernels: 70 us -> 54.1 us  [local(): pl.pallas_call(kernel, out_shape=(jax.ShapeDtypeStruct((PATHS, COLS), F32...]
    unnamed x13 -> x14, local copies, waits for them, and re-layouts: 6.78 us -> 6.66 us
where the time goes in v2:
time: 61.8 us; the launch traced here: 61.4 us
  Pallas kernels  54.1 us (88%)
  local copies, waits for them, and re-layouts  6.66 us (11%)
  between operations  0.65 us (1%)
    pallas_call x1, Pallas kernels, local(): pl.pallas_call(kernel, out_shape=(jax.ShapeDtypeStruct((PATHS, COLS), F32...  54.1 us
    unnamed x14, local copies, waits for them, and re-layouts  6.66 us

profile of v2, /device:TPU:1, one launch (start us, length us, event | category | flops | bytes accessed | tf_op | source)
XLA Modules:
  0.0 61.4 jit_solution(2558628590601749159)
XLA Ops:
  0.6 0.0 copy-start
  0.6 0.8 %copy-done = f32[16384]{0:T(1024)S(1)} copy-done((f32[16384]{0:T(1024)S(1)}, f32[16384]{0:T(1024)}, u32[]{:S(2)}) %copy-start) | copy-done | bytes 65560
  1.5 0.0 copy-start.1
  1.5 0.8 %copy-done.1 = s32[16384]{0:T(1024)S(1)} copy-done((s32[16384]{0:T(1024)S(1)}, s32[16384]{0:T(1024)}, u32[]{:S(2)}) %copy-start.1) | copy-done | bytes 65560
  2.3 0.0 copy-start.2
  2.3 0.8 %copy-done.2 = s32[16384]{0:T(1024)S(1)} copy-done((s32[16384]{0:T(1024)S(1)}, s32[16384]{0:T(1024)}, u32[]{:S(2)}) %copy-start.2) | copy-done | bytes 65560
  3.2 0.0 copy-start.3
  3.2 0.8 %copy-done.3 = s32[16384]{0:T(1024)S(1)} copy-done((s32[16384]{0:T(1024)S(1)}, s32[16384]{0:T(1024)}, u32[]{:S(2)}) %copy-start.3) | copy-done | bytes 65560
  4.0 0.0 copy-start.4
  4.0 0.7 %copy-done.4 = bf16[256,32]{0,1:T(8,128)(2,1)S(1)} copy-done((bf16[256,32]{0,1:T(8,128)(2,1)S(1)}, bf16[256,32]{0,1:T(8,128)(2,1)}, u32[]{:S(2)}) %copy-start.4) | copy-done | bytes 16408
  4.7 0.0 copy-start.5
  4.7 0.7 %copy-done.5 = f32[32]{0:T(128)S(1)} copy-done((f32[32]{0:T(128)S(1)}, f32[32]{0:T(128)}, u32[]{:S(2)}) %copy-start.5) | copy-done | bytes 152
  5.4 54.1 %shard_map.86 = (f32[32,256]{1,0:T(8,128)S(1)}, f32[32,16384]{1,0:T(8,128)S(1)}) custom-call(bf16[16384,256]{1,0:T(8,128)(2,1)} %design.1, bf16[32,256]{1,0:T(8,128)(2,1)S(1)} %bitcast.12, f32[1,32]{1,0:T(1,128)S(1)} %bitcast.13, f32[128,128]{1,0:T(8,128)S(1)} %bitcast.7, s32[128,128]{1,0:T(8,128)S(1)} %bitcast.8, s32[128,128]{1,0:T(8,128)S(1)} %bitcast.9, ...), custom_call_target="tpu_custom_call" | custom-call | flops 536870912 | bytes 10485760 | tf_op jit(solution)/shard_map/pallas_call | solution.py:367
  59.5 0.6 %copy.11 = f32[256,32]{0,1:T(8,128)} copy(f32[256,32]{0,1:T(8,128)S(1)} %bitcast.11) | data formatting | bytes 65536
  60.1 1.3 %copy.12 = f32[32,16384]{1,0:T(8,128)} copy(f32[32,16384]{1,0:T(8,128)S(1)} %get-tuple-element.9) | data formatting | bytes 4194304
Async XLA Ops:
  0.6 0.8 %copy-start = (f32[16384]{0:T(1024)S(1)}, f32[16384]{0:T(1024)}, u32[]{:S(2)}) copy-start(f32[16384]{0:T(1024)} %param.10) | copy-start | bytes 196612
  1.5 0.8 %copy-start.1 = (s32[16384]{0:T(1024)S(1)}, s32[16384]{0:T(1024)}, u32[]{:S(2)}) copy-start(s32[16384]{0:T(1024)} %param.11) | copy-start | bytes 196612
  2.3 0.8 %copy-start.2 = (s32[16384]{0:T(1024)S(1)}, s32[16384]{0:T(1024)}, u32[]{:S(2)}) copy-start(s32[16384]{0:T(1024)} %param.12) | copy-start | bytes 196612
  3.2 0.8 %copy-start.3 = (s32[16384]{0:T(1024)S(1)}, s32[16384]{0:T(1024)}, u32[]{:S(2)}) copy-start(s32[16384]{0:T(1024)} %param.13) | copy-start | bytes 196612
  4.0 0.7 %copy-start.4 = (bf16[256,32]{0,1:T(8,128)(2,1)S(1)}, bf16[256,32]{0,1:T(8,128)(2,1)}, u32[]{:S(2)}) copy-start(bf16[256,32]{0,1:T(8,128)(2,1)} %param.8) | copy-start | bytes 49156
  4.7 0.7 %copy-start.5 = (f32[32]{0:T(128)S(1)}, f32[32]{0:T(128)}, u32[]{:S(2)}) copy-start(f32[32]{0:T(128)} %param.9) | copy-start | bytes 388

commit v3 on v2

--- a/solution.py
+++ b/solution.py
@@ -21,7 +21,6 @@
 QUART = BLOCKS // 4
 CHUNK = ROWS // 4
 TILE1 = 4096
-TILE2 = 4096
 NBATCH = 2
 
 
@@ -71,8 +70,8 @@
 def kernel(
     design, coefs, penalty, censor, codes, first, last,
     new_out, weights_out,
-    D, C, PEN, CEN, COD, FST, LST, IC2, E, R1, R2, S, R4, ETA, EX, BASE, TS, TR, W, SP, SR, SUM,
-    load_sem, send_sem, recv_sem,
+    D, C, PEN, CEN, COD, FST, LST, IC2, E, R1, R2, S, R4, ETA, EX, BASE, TS, TR, W, SP, SR, SUM, OUTV,
+    load_sem, out_sem, send_sem, recv_sem,
 ):
     s = lax.axis_index("subj")
     cov = lax.axis_index("cov")
@@ -115,6 +114,12 @@
     def received(*group):
         at, rows = groups[group]
         wait_rows(recv_sem.at[at], rows)
+
+    barrier = pltpu.get_barrier_semaphore()
+    peers = [device(axis, at) for axis in (0, 1) for at in ring(axis)]
+    peers += [((s + d) % SUBJ, cov) for d in range(1, SUBJ)]
+    for peer in peers:
+        pl.semaphore_signal(barrier, inc=1, device_id=peer, device_id_type=MESH)
 
     order = (0, 2, 1, 3)
     chunks = {}
@@ -132,12 +137,6 @@
     for copy in small[1:]:
         copy.start()
 
-    barrier = pltpu.get_barrier_semaphore()
-    peers = [device(axis, at) for axis in (0, 1) for at in ring(axis)]
-    peers += [((s + d) % SUBJ, cov) for d in range(1, SUBJ)]
-    for peer in peers:
-        pl.semaphore_signal(barrier, inc=1, device_id=peer, device_id_type=MESH)
-
     small[0].wait()
     nt = (((1,), (1,)), ((), ()))
     lhs = C[...]
@@ -246,40 +245,46 @@
         event = jnp.where(COD[...] == 1, 1.0, 0.0)
         W5[x, z, k] = event - EX[k] * (BASE[k] + (early_in + IC2[...] * later_in))
 
-    def spot(h, k, at):
-        rows = pl.ds(h * HALF, HALF)
-        return W5.at[x, at, k, rows, :] if h == 0 else W5.at[at, z, k, rows, :]
-
-    def ag_first(h, k):
-        mine = spot(h, k, pos[1 - h])
+    def ag_first(h, k, part):
+        start = part * QUART
+        rows = pl.ds(h * HALF + start, QUART)
+        mine = W5.at[x, z, k, rows, :]
         for at in ring(1 - h):
-            send(("a1", h, k), mine, mine, device(1 - h, at))
-        for at in ring(h):
-            send(("a2", h, k), mine, mine, device(h, at))
-
-    def ag_second(h, k):
-        received("a1", h, k)
-        for came in ring(1 - h):
-            piece = spot(h, k, came)
-            for at in ring(h):
-                send(("a2", h, k), piece, piece, device(h, at))
-
-    def ag_end(h, k):
-        received("a2", h, k)
-
-    def score(k):
-        total = jnp.zeros((PATHS // 2, COLS), F32)
-        for i in range(ROWS // TILE2):
-            start = i * TILE2
+            send(("a1", h, k, part), mine, mine, device(1 - h, at))
+
+    def ag_second(h, k, part):
+        received("a1", h, k, part)
+        left, right, opposite = ring(h)
+        mine = quarter(W5, h, pos[h], k, part * QUART, QUART)
+        for at in (left, right):
+            send(("a2", h, k, part), mine, mine, device(h, at))
+
+    def ag_third(h, k, part):
+        left, right, opposite = ring(h)
+        received("a2", h, k, part)
+        for came, to, start in ((left, right, 0), (right, left, QUART // 2)):
+            piece = quarter(W5, h, came, k, part * QUART + start, QUART // 2)
+            send(("a3", h, k, part), piece, piece, device(h, to))
+
+    def ag_end(h, k, part):
+        received("a3", h, k, part)
+
+    def score(k, part, total):
+        def body(h, total):
+            start = pl.multiple_of((2 * h + part) * CHUNK, CHUNK)
             parts = []
-            for j in range(TILE2 // LANES):
-                block = start // LANES + j
+            for j in range(QUART):
+                block = (2 * h + part) * QUART + j
                 rows = [
                     W[pl.ds((g * 16 + k) * BLOCKS + block, 8, stride=2 * BLOCKS), :]
                     for g in range(2)
                 ]
                 parts.append(jnp.concatenate(rows, axis=0).astype(BF16))
-            total = total + dot(jnp.concatenate(parts, axis=1), D[start : start + TILE2, :])
+            return total + dot(jnp.concatenate(parts, axis=1), D[pl.ds(start, CHUNK), :])
+
+        return lax.fori_loop(0, 2, body, total)
+
+    def score_out(k, total):
         SP[k] = total
         for d in range(1, SUBJ):
             send(("s", k), SP.at[k], SR.at[k, s], ((s + d) % SUBJ, cov))
@@ -317,23 +322,37 @@
         scan_b(k)
     for k in both:
         scan_c(k)
-        for h in both:
-            ag_first(h, k)
+        for part in both:
+            for h in both:
+                ag_first(h, k, part)
+    for step in (ag_second, ag_third):
+        for k in both:
+            for part in both:
+                for h in both:
+                    step(h, k, part)
     for k in both:
-        for h in both:
-            ag_second(h, k)
-    for h in both:
-        ag_end(h, 0)
-    score(0)
-    for h in both:
-        ag_end(h, 1)
-    score(1)
-
-    for block in range(BLOCKS):
-        for g in range(4):
-            weights_out[g * 8 : g * 8 + 8, block * LANES : (block + 1) * LANES] = W[
-                pl.ds(g * 8 * BLOCKS + block, 8, stride=BLOCKS), :
-            ]
+        total = jnp.zeros((PATHS // 2, COLS), F32)
+        for part in both:
+            for h in both:
+                ag_end(h, k, part)
+            total = score(k, part, total)
+        score_out(k, total)
+    outs = []
+    for c in range(4):
+        part = pl.ds(c * CHUNK, CHUNK)
+
+        def convert(block, carry):
+            lanes = pl.ds(pl.multiple_of(block * LANES, LANES), LANES)
+            for g in range(4):
+                OUTV[g * 8 : g * 8 + 8, lanes] = W[
+                    pl.ds(g * 8 * BLOCKS + block, 8, stride=BLOCKS), :
+                ]
+            return carry
+
+        lax.fori_loop(c * QUART, (c + 1) * QUART, convert, 0, unroll=8)
+        copy = pltpu.make_async_copy(OUTV.at[:, part], weights_out.at[:, part], out_sem.at[c])
+        copy.start()
+        outs.append(copy)
     eye = (
         lax.broadcasted_iota(jnp.int32, (PATHS, PATHS), 0)
         == lax.broadcasted_iota(jnp.int32, (PATHS, PATHS), 1)
@@ -355,9 +374,27 @@
         shifted = wide[:, cols] + scale * SUM[c]
         sign = jnp.where(shifted > 0, 1.0, jnp.where(shifted < 0, -1.0, 0.0))
         new_out[:, cols] = sign * jnp.maximum(jnp.abs(shifted) - limit, 0.0)
+    for copy in outs:
+        copy.wait()
     left_rows = sent_rows[0]
     span = D.at[pl.ds(0, left_rows), :]
     pltpu.make_async_copy(span, span, send_sem.at[0]).wait()
+
+
+def hand_over(new, weights, new_out, weights_out, N, V, in_sem, out_sem):
+    parts = [(new, N, new_out)]
+    for c in range(4):
+        part = pl.ds(c * CHUNK, CHUNK)
+        parts.append((weights.at[:, part], V.at[:, part], weights_out.at[:, part]))
+    ins = [pltpu.make_async_copy(a, b, in_sem.at[i]) for i, (a, b, c) in enumerate(parts)]
+    outs = [pltpu.make_async_copy(b, c, out_sem.at[i]) for i, (a, b, c) in enumerate(parts)]
+    for copy in ins:
+        copy.start()
+    for come, go in zip(ins, outs):
+        come.wait()
+        go.start()
+    for go in outs:
+        go.wait()
 
 
 def local(design, coefs, penalty, censor, codes, tie_first, tie_last):
@@ -371,7 +408,7 @@
             jax.ShapeDtypeStruct((PATHS, ROWS), F32),
         ),
         in_specs=[pl.BlockSpec(memory_space=pltpu.HBM)] * 7,
-        out_specs=(pl.BlockSpec(memory_space=pltpu.VMEM), pl.BlockSpec(memory_space=pltpu.VMEM)),
+        out_specs=(pl.BlockSpec(memory_space=pltpu.VMEM), pl.BlockSpec(memory_space=pltpu.HBM)),
         scratch_shapes=[
             vmem((ROWS, COLS), BF16),
             vmem((PATHS, COLS), BF16),
@@ -395,12 +432,14 @@
             vmem((NBATCH, PATHS // 2, COLS), F32),
             vmem((NBATCH, SUBJ, PATHS // 2, COLS), F32),
             vmem((2, PATHS, LANES), F32),
+            vmem((PATHS, ROWS), F32),
             dma((10,)),
+            dma((4,)),
             dma((1,)),
-            dma((26,)),
+            dma((42,)),
         ],
         compiler_params=pltpu.CompilerParams(
-            collective_id=0, has_side_effects=True, vmem_limit_bytes=48 * 2**20
+            collective_id=0, has_side_effects=True, vmem_limit_bytes=56 * 2**20
         ),
         cost_estimate=pl.CostEstimate(
             flops=4 * PATHS * ROWS * COLS,
@@ -416,6 +455,22 @@
         tie_first.reshape(square),
         tie_last.reshape(square),
     )
+    new, weights = pl.pallas_call(
+        hand_over,
+        out_shape=(
+            jax.ShapeDtypeStruct((PATHS, COLS), F32),
+            jax.ShapeDtypeStruct((PATHS, ROWS), F32),
+        ),
+        in_specs=[pl.BlockSpec(memory_space=pltpu.HBM)] * 2,
+        out_specs=(pl.BlockSpec(memory_space=pltpu.HBM), pl.BlockSpec(memory_space=pltpu.HBM)),
+        scratch_shapes=[
+            vmem((PATHS, COLS), F32),
+            vmem((PATHS, ROWS), F32),
+            dma((5,)),
+            dma((5,)),
+        ],
+        compiler_params=pltpu.CompilerParams(vmem_limit_bytes=60 * 2**20),
+    )(new, weights)
     return new.T, weights
 
 

time: 61.8 us -> 56 us (0.906)
  local copies, waits for them, and re-layouts: 6.66 us -> 0 us
  Pallas kernels: 54.1 us -> 55.2 us
    unnamed x14 -> x0, local copies, waits for them, and re-layouts: 6.66 us -> none
    pallas_call x0 -> x1, Pallas kernels: none -> 2.46 us  [local(): pl.pallas_call(hand_over, out_shape=(jax.ShapeDtypeStruct((PATHS, COLS),...]
    pallas_call x1, Pallas kernels: 54.1 us -> 52.8 us  [local(): pl.pallas_call(kernel, out_shape=(jax.ShapeDtypeStruct((PATHS, COLS), F32...]
where the time goes in v3:
time: 56 us; the launch traced here: 55.9 us
  Pallas kernels  55.2 us (99%)
  between operations  0.64 us (1%)
    pallas_call x1, Pallas kernels, local(): pl.pallas_call(kernel, out_shape=(jax.ShapeDtypeStruct((PATHS, COLS), F32...  52.8 us
    pallas_call x1, Pallas kernels, local(): pl.pallas_call(hand_over, out_shape=(jax.ShapeDtypeStruct((PATHS, COLS),...  2.46 us

profile of v3, /device:TPU:1, one launch (start us, length us, event | category | flops | bytes accessed | tf_op | source)
XLA Modules:
  0.0 55.9 jit_solution(12598686023791478849)
XLA Ops:
  0.6 52.8 %shard_map.86 = (f32[32,256]{1,0:T(8,128)}, f32[32,16384]{1,0:T(8,128)}) custom-call(bf16[16384,256]{1,0:T(8,128)(2,1)} %design.1, bf16[32,256]{1,0:T(8,128)(2,1)} %bitcast.11, f32[1,32]{1,0:T(1,128)} %bitcast.12, f32[128,128]{1,0:T(8,128)} %bitcast.7, s32[128,128]{1,0:T(8,128)} %bitcast.8, s32[128,128]{1,0:T(8,128)} %bitcast.9, s32[128,128]{1,0:T(8,128)} %bitcast.10), custom_call_target="tpu_custom_call" | custom-call | flops 536870912 | bytes 10485760 | tf_op jit(solution)/shard_map/pallas_call | solution.py:404
  53.4 2.5 %shard_map.87 = (f32[32,256]{1,0:T(8,128)}, f32[32,16384]{1,0:T(8,128)}) custom-call(f32[32,256]{1,0:T(8,128)} %get-tuple-element.6.new, f32[32,16384]{1,0:T(8,128)} %get-tuple-element.7.weights), custom_call_target="tpu_custom_call" | custom-call | tf_op jit(solution)/shard_map/pallas_call | solution.py:458

commit v4 on v3

--- a/solution.py
+++ b/solution.py
@@ -19,9 +19,11 @@
 BLOCKS = ROWS // LANES
 HALF = BLOCKS // 2
 QUART = BLOCKS // 4
+EIGHTH = BLOCKS // 8
 CHUNK = ROWS // 4
-TILE1 = 4096
 NBATCH = 2
+CHUNKS = ((0, 0, 16), (1, 0, 16), (0, 16, 16), (1, 16, 16), (0, 32, 16), (1, 32, 16), (0, 48, 16), (1, 48, 16))
+FAR_FIRST = (4, 3, 5, 2, 6, 1, 7)
 
 
 def split3(x):
@@ -108,7 +110,7 @@
         ).start()
 
     def wait_rows(sem, rows):
-        span = W.at[pl.ds(0, rows), :] if rows <= PATHS * BLOCKS else None
+        span = W.at[pl.ds(0, rows), :]
         pltpu.make_async_copy(span, span, sem).wait()
 
     def received(*group):
@@ -121,19 +123,18 @@
     for peer in peers:
         pl.semaphore_signal(barrier, inc=1, device_id=peer, device_id_type=MESH)
 
-    order = (0, 2, 1, 3)
-    chunks = {}
-    for i in order:
-        part = pl.ds(i * CHUNK, CHUNK)
-        chunks[i] = pltpu.make_async_copy(design.at[part], D.at[part], load_sem.at[i])
+    chunks = []
+    for i, (h, first_block, blocks) in enumerate(CHUNKS):
+        part = pl.ds((h * HALF + first_block) * LANES, blocks * LANES)
+        chunks.append(pltpu.make_async_copy(design.at[part], D.at[part], load_sem.at[i]))
     small = []
     for i, (src, dst) in enumerate(
         [(coefs, C), (penalty, PEN), (censor, CEN), (codes, COD), (first, FST), (last, LST)]
     ):
-        small.append(pltpu.make_async_copy(src, dst, load_sem.at[4 + i]))
+        small.append(pltpu.make_async_copy(src, dst, load_sem.at[len(CHUNKS) + i]))
     small[0].start()
-    for i in order:
-        chunks[i].start()
+    for copy in chunks:
+        copy.start()
     for copy in small[1:]:
         copy.start()
 
@@ -141,49 +142,67 @@
     nt = (((1,), (1,)), ((), ()))
     lhs = C[...]
 
-    def predict(chunk):
-        for i in range(CHUNK // TILE1):
-            start = chunk * CHUNK + i * TILE1
-            part = lax.dot_general(lhs, D[start : start + TILE1, :], nt, preferred_element_type=F32)
-            for j in range(TILE1 // LANES):
-                block = start // LANES + j
-                for g in range(4):
-                    E[pl.ds(g * 8 * BLOCKS + block, 8, stride=BLOCKS), :] = part[
-                        g * 8 : g * 8 + 8, j * LANES : (j + 1) * LANES
-                    ]
+    def predict(h, first_block, blocks):
+        start = (h * HALF + first_block) * LANES
+        part = lax.dot_general(
+            lhs, D[start : start + blocks * LANES, :], nt, preferred_element_type=F32
+        )
+        for j in range(blocks):
+            block = h * HALF + first_block + j
+            for g in range(4):
+                E[pl.ds(g * 8 * BLOCKS + block, 8, stride=BLOCKS), :] = part[
+                    g * 8 : g * 8 + 8, j * LANES : (j + 1) * LANES
+                ]
 
     def quarter(ref, half, at, k, start, size):
         rows = pl.ds(half * HALF + start, size)
         return ref.at[at, :, k, rows, :] if half == 0 else ref.at[:, at, k, rows, :]
 
-    def rs_far(h, k, part):
+    def rs_far(h, k, part, d):
         left, right, opposite = ring(h)
-        start, d, to = ((0, 0, right), (QUART, 1, left))[part]
-        send(("m1", h, k), quarter(E5, h, opposite, k, start, QUART), R1.at[h, k, d], device(h, to))
-
-    def rs_near(h, k, part):
+        start = part * QUART + d * EIGHTH
+        send(
+            ("m1", h, k, part),
+            quarter(E5, h, opposite, k, start, EIGHTH),
+            R1.at[h, k, part, d],
+            device(h, left if d else right),
+        )
+
+    def rs_near(h, k, part, d):
         left, right, opposite = ring(h)
-        start, d, to = ((0, 1, left), (QUART, 0, right))[part]
+        start = part * QUART + d * EIGHTH
+        to = right if d else left
         send(
-            ("m2", h, k),
-            quarter(E5, h, to, k, start, QUART),
-            R2.at[h, k, d, :, pl.ds(start, QUART), :],
+            ("m2", h, k, part),
+            quarter(E5, h, to, k, start, EIGHTH),
+            R2.at[h, k, 1 - d, :, pl.ds(start, EIGHTH), :],
             device(h, to),
         )
 
-    def rs_on(h, k):
+    def rs_on(h, k, part):
         left, right, opposite = ring(h)
-        received("m1", h, k)
-        for d, to, start in ((0, right, 0), (1, left, QUART)):
-            mine = quarter(E5, h, to, k, start, QUART)
-            mine[...] = mine[...] + R1[h, k, d]
-            send(("m2", h, k), mine, R2.at[h, k, d, :, pl.ds(start, QUART), :], device(h, to))
-
-    def rs_second(h, k):
-        received("m2", h, k)
-        S[h, k] = quarter(E5, h, pos[h], k, 0, HALF)[...] + R2[h, k, 0] + R2[h, k, 1]
-        for slot, at in enumerate(ring(1 - h)):
-            send(("n", h, k), S.at[h, k, at], R4.at[h, k, slot], device(1 - h, at))
+        received("m1", h, k, part)
+        for d, to in ((0, right), (1, left)):
+            start = part * QUART + d * EIGHTH
+            mine = quarter(E5, h, to, k, start, EIGHTH)
+            mine[...] = mine[...] + R1[h, k, part, d]
+            send(
+                ("m2", h, k, part),
+                mine,
+                R2.at[h, k, d, :, pl.ds(start, EIGHTH), :],
+                device(h, to),
+            )
+
+    def rs_second(h, k, part):
+        received("m2", h, k, part)
+        rows = pl.ds(part * QUART, QUART)
+        S[h, k, :, rows, :] = (
+            quarter(E5, h, pos[h], k, part * QUART, QUART)[...]
+            + R2[h, k, 0, :, rows, :]
+            + R2[h, k, 1, :, rows, :]
+        )
+        for slot, at in reversed(list(enumerate(ring(1 - h)))):
+            send(("n", h, k), S.at[h, k, at, rows, :], R4.at[h, k, slot, rows, :], device(1 - h, at))
 
     def rs_end(h, k):
         received("n", h, k)
@@ -192,7 +211,7 @@
         )
 
     def exchange(k, e):
-        for d in range(1, SUBJ):
+        for d in FAR_FIRST:
             send(("t", k, e), TS.at[k, e], TR.at[k, e, d], ((s + d) % SUBJ, cov))
 
     def arrived(k, e):
@@ -249,7 +268,7 @@
         start = part * QUART
         rows = pl.ds(h * HALF + start, QUART)
         mine = W5.at[x, z, k, rows, :]
-        for at in ring(1 - h):
+        for at in reversed(ring(1 - h)):
             send(("a1", h, k, part), mine, mine, device(1 - h, at))
 
     def ag_second(h, k, part):
@@ -286,32 +305,45 @@
 
     def score_out(k, total):
         SP[k] = total
-        for d in range(1, SUBJ):
+        for d in FAR_FIRST:
             send(("s", k), SP.at[k], SR.at[k, s], ((s + d) % SUBJ, cov))
         SR[k, s] = total
 
     both = (0, 1)
-    for i, (chunk, h, part) in enumerate(((0, 0, 0), (2, 1, 0), (1, 0, 1), (3, 1, 1))):
-        chunks[chunk].wait()
-        predict(chunk)
+    both = (0, 1)
+    for i, (h, first_block, blocks) in enumerate(CHUNKS):
+        chunks[i].wait()
+        predict(h, first_block, blocks)
         if i == 0:
             pl.semaphore_wait(barrier, len(peers))
-        rs_far(h, 0, part)
-        rs_near(h, 0, part)
-    for h in both:
-        rs_far(h, 1, 0)
-        rs_far(h, 1, 1)
-    for h in both:
-        rs_on(h, 0)
-    for h in both:
-        rs_near(h, 1, 0)
-        rs_near(h, 1, 1)
+        for at in range(first_block // EIGHTH, (first_block + blocks) // EIGHTH):
+            part, d = at // 2, at % 2
+            rs_far(h, 0, part, d)
+            rs_near(h, 0, part, d)
+            rs_far(h, 1, part, d)
+    for h in both:
+        rs_on(h, 0, 0)
+    for h in both:
+        for d in both:
+            rs_near(h, 1, 0, d)
+    for h in both:
+        rs_on(h, 0, 1)
+    for h in both:
+        for d in both:
+            rs_near(h, 1, 1, d)
     prepare()
     for h in both:
-        rs_on(h, 1)
-    for k in both:
-        for h in both:
-            rs_second(h, k)
+        rs_on(h, 1, 0)
+    for h in both:
+        rs_second(h, 0, 0)
+    for h in both:
+        rs_on(h, 1, 1)
+    for h in both:
+        rs_second(h, 0, 1)
+    for h in both:
+        rs_second(h, 1, 0)
+    for h in both:
+        rs_second(h, 1, 1)
     for h in both:
         rs_end(h, 0)
     scan_a(0)
@@ -419,7 +451,7 @@
             vmem(square, jnp.int32),
             vmem(square, F32),
             vmem((PATHS * BLOCKS, LANES), F32),
-            vmem((2, NBATCH, 2, RING, QUART, LANES), F32),
+            vmem((2, NBATCH, 2, 2, RING, EIGHTH, LANES), F32),
             vmem((2, NBATCH, 2, RING, HALF, LANES), F32),
             vmem((2, NBATCH, RING, HALF, LANES), F32),
             vmem((2, NBATCH, 3, HALF, LANES), F32),
@@ -433,10 +465,10 @@
             vmem((NBATCH, SUBJ, PATHS // 2, COLS), F32),
             vmem((2, PATHS, LANES), F32),
             vmem((PATHS, ROWS), F32),
-            dma((10,)),
+            dma((len(CHUNKS) + 6,)),
             dma((4,)),
             dma((1,)),
-            dma((42,)),
+            dma((50,)),
         ],
         compiler_params=pltpu.CompilerParams(
             collective_id=0, has_side_effects=True, vmem_limit_bytes=56 * 2**20

time: 56 us -> 54.3 us (0.970)
  Pallas kernels: 55.2 us -> 53.5 us
    pallas_call x1, Pallas kernels: 52.8 us -> 51.1 us  [local(): pl.pallas_call(kernel, out_shape=(jax.ShapeDtypeStruct((PATHS, COLS), F32...]
where the time goes in v4:
time: 54.3 us; the launch traced here: 54.2 us
  Pallas kernels  53.5 us (99%)
  between operations  0.64 us (1%)
    pallas_call x1, Pallas kernels, local(): pl.pallas_call(kernel, out_shape=(jax.ShapeDtypeStruct((PATHS, COLS), F32...  51.1 us
    pallas_call x1, Pallas kernels, local(): pl.pallas_call(hand_over, out_shape=(jax.ShapeDtypeStruct((PATHS, COLS),...  2.46 us

profile of v4, /device:TPU:1, one launch (start us, length us, event | category | flops | bytes accessed | tf_op | source)
XLA Modules:
  0.0 54.2 jit_solution(8445251521304273340)
XLA Ops:
  0.6 51.1 %shard_map.86 = (f32[32,256]{1,0:T(8,128)}, f32[32,16384]{1,0:T(8,128)}) custom-call(bf16[16384,256]{1,0:T(8,128)(2,1)} %design.1, bf16[32,256]{1,0:T(8,128)(2,1)} %bitcast.11, f32[1,32]{1,0:T(1,128)} %bitcast.12, f32[128,128]{1,0:T(8,128)} %bitcast.7, s32[128,128]{1,0:T(8,128)} %bitcast.8, s32[128,128]{1,0:T(8,128)} %bitcast.9, s32[128,128]{1,0:T(8,128)} %bitcast.10), custom_call_target="tpu_custom_call" | custom-call | flops 536870912 | bytes 10485760 | tf_op jit(solution)/shard_map/pallas_call | solution.py:436
  51.7 2.5 %shard_map.87 = (f32[32,256]{1,0:T(8,128)}, f32[32,16384]{1,0:T(8,128)}) custom-call(f32[32,256]{1,0:T(8,128)} %get-tuple-element.6.new, f32[32,16384]{1,0:T(8,128)} %get-tuple-element.7.weights), custom_call_target="tpu_custom_call" | custom-call | tf_op jit(solution)/shard_map/pallas_call | solution.py:490

commit v5 on v4

--- a/solution.py
+++ b/solution.py
@@ -72,8 +72,8 @@
 def kernel(
     design, coefs, penalty, censor, codes, first, last,
     new_out, weights_out,
-    D, C, PEN, CEN, COD, FST, LST, IC2, E, R1, R2, S, R4, ETA, EX, BASE, TS, TR, W, SP, SR, SUM, OUTV,
-    load_sem, out_sem, send_sem, recv_sem,
+    D, C, PEN, CEN, COD, FST, LST, IC2, E, R1, R2, S, R4, ETA, EX, BASE, TS, TR, W, SP, SR, SUM,
+    load_sem, send_sem, recv_sem,
 ):
     s = lax.axis_index("subj")
     cov = lax.axis_index("cov")
@@ -369,22 +369,16 @@
                 ag_end(h, k, part)
             total = score(k, part, total)
         score_out(k, total)
-    outs = []
-    for c in range(4):
-        part = pl.ds(c * CHUNK, CHUNK)
-
-        def convert(block, carry):
-            lanes = pl.ds(pl.multiple_of(block * LANES, LANES), LANES)
-            for g in range(4):
-                OUTV[g * 8 : g * 8 + 8, lanes] = W[
-                    pl.ds(g * 8 * BLOCKS + block, 8, stride=BLOCKS), :
-                ]
-            return carry
-
-        lax.fori_loop(c * QUART, (c + 1) * QUART, convert, 0, unroll=8)
-        copy = pltpu.make_async_copy(OUTV.at[:, part], weights_out.at[:, part], out_sem.at[c])
-        copy.start()
-        outs.append(copy)
+
+    def convert(block, carry):
+        lanes = pl.ds(pl.multiple_of(block * LANES, LANES), LANES)
+        for g in range(4):
+            weights_out[g * 8 : g * 8 + 8, lanes] = W[
+                pl.ds(g * 8 * BLOCKS + block, 8, stride=BLOCKS), :
+            ]
+        return carry
+
+    lax.fori_loop(0, BLOCKS, convert, 0, unroll=8)
     eye = (
         lax.broadcasted_iota(jnp.int32, (PATHS, PATHS), 0)
         == lax.broadcasted_iota(jnp.int32, (PATHS, PATHS), 1)
@@ -406,27 +400,20 @@
         shifted = wide[:, cols] + scale * SUM[c]
         sign = jnp.where(shifted > 0, 1.0, jnp.where(shifted < 0, -1.0, 0.0))
         new_out[:, cols] = sign * jnp.maximum(jnp.abs(shifted) - limit, 0.0)
-    for copy in outs:
-        copy.wait()
     left_rows = sent_rows[0]
     span = D.at[pl.ds(0, left_rows), :]
     pltpu.make_async_copy(span, span, send_sem.at[0]).wait()
 
 
-def hand_over(new, weights, new_out, weights_out, N, V, in_sem, out_sem):
-    parts = [(new, N, new_out)]
+def hand_over(new, weights, new_out, weights_out, sem):
+    copies = [pltpu.make_async_copy(new, new_out, sem.at[4])]
     for c in range(4):
-        part = pl.ds(c * CHUNK, CHUNK)
-        parts.append((weights.at[:, part], V.at[:, part], weights_out.at[:, part]))
-    ins = [pltpu.make_async_copy(a, b, in_sem.at[i]) for i, (a, b, c) in enumerate(parts)]
-    outs = [pltpu.make_async_copy(b, c, out_sem.at[i]) for i, (a, b, c) in enumerate(parts)]
-    for copy in ins:
+        rows = pl.ds(c * 8, 8)
+        copies.append(pltpu.make_async_copy(weights.at[rows], weights_out.at[rows], sem.at[c]))
+    for copy in copies:
         copy.start()
-    for come, go in zip(ins, outs):
-        come.wait()
-        go.start()
-    for go in outs:
-        go.wait()
+    for copy in copies:
+        copy.wait()
 
 
 def local(design, coefs, penalty, censor, codes, tie_first, tie_last):
@@ -440,7 +427,7 @@
             jax.ShapeDtypeStruct((PATHS, ROWS), F32),
         ),
         in_specs=[pl.BlockSpec(memory_space=pltpu.HBM)] * 7,
-        out_specs=(pl.BlockSpec(memory_space=pltpu.VMEM), pl.BlockSpec(memory_space=pltpu.HBM)),
+        out_specs=(pl.BlockSpec(memory_space=pltpu.VMEM), pl.BlockSpec(memory_space=pltpu.VMEM)),
         scratch_shapes=[
             vmem((ROWS, COLS), BF16),
             vmem((PATHS, COLS), BF16),
@@ -464,14 +451,12 @@
             vmem((NBATCH, PATHS // 2, COLS), F32),
             vmem((NBATCH, SUBJ, PATHS // 2, COLS), F32),
             vmem((2, PATHS, LANES), F32),
-            vmem((PATHS, ROWS), F32),
             dma((len(CHUNKS) + 6,)),
-            dma((4,)),
             dma((1,)),
             dma((50,)),
         ],
         compiler_params=pltpu.CompilerParams(
-            collective_id=0, has_side_effects=True, vmem_limit_bytes=56 * 2**20
+            collective_id=0, has_side_effects=True, vmem_limit_bytes=48 * 2**20
         ),
         cost_estimate=pl.CostEstimate(
             flops=4 * PATHS * ROWS * COLS,
@@ -479,13 +464,18 @@
             transcendentals=2 * ROWS,
         ),
     )(
-        design,
-        coefs.T,
-        penalty.reshape(1, PATHS),
-        censor.reshape(square),
-        codes.reshape(square),
-        tie_first.reshape(square),
-        tie_last.reshape(square),
+        *(
+            pltpu.with_memory_space_constraint(a, pltpu.HBM)
+            for a in (
+                design,
+                coefs.T,
+                penalty.reshape(1, PATHS),
+                censor.reshape(square),
+                codes.reshape(square),
+                tie_first.reshape(square),
+                tie_last.reshape(square),
+            )
+        )
     )
     new, weights = pl.pallas_call(
         hand_over,
@@ -493,15 +483,10 @@
             jax.ShapeDtypeStruct((PATHS, COLS), F32),
             jax.ShapeDtypeStruct((PATHS, ROWS), F32),
         ),
-        in_specs=[pl.BlockSpec(memory_space=pltpu.HBM)] * 2,
+        in_specs=[pl.BlockSpec(memory_space=pltpu.VMEM)] * 2,
         out_specs=(pl.BlockSpec(memory_space=pltpu.HBM), pl.BlockSpec(memory_space=pltpu.HBM)),
-        scratch_shapes=[
-            vmem((PATHS, COLS), F32),
-            vmem((PATHS, ROWS), F32),
-            dma((5,)),
-            dma((5,)),
-        ],
-        compiler_params=pltpu.CompilerParams(vmem_limit_bytes=60 * 2**20),
+        scratch_shapes=[dma((5,))],
+        compiler_params=pltpu.CompilerParams(vmem_limit_bytes=40 * 2**20),
     )(new, weights)
     return new.T, weights
 

time: 54.3 us -> 52.6 us (0.969)
  Pallas kernels: 53.5 us -> 51.8 us
    pallas_call x1, Pallas kernels: 2.46 us -> 1.37 us  [local(): pl.pallas_call(hand_over, out_shape=(jax.ShapeDtypeStruct((PATHS, COLS),...]
    pallas_call x1, Pallas kernels: 51.1 us -> 50.4 us  [local(): pl.pallas_call(kernel, out_shape=(jax.ShapeDtypeStruct((PATHS, COLS), F32...]
where the time goes in v5:
time: 52.6 us; the launch traced here: 52.4 us
  Pallas kernels  51.8 us (98%)
  between operations  0.64 us (1%)
    pallas_call x1, Pallas kernels, local(): pl.pallas_call(kernel, out_shape=(jax.ShapeDtypeStruct((PATHS, COLS), F32...  50.4 us
    pallas_call x1, Pallas kernels, local(): pl.pallas_call(hand_over, out_shape=(jax.ShapeDtypeStruct((PATHS, COLS),...  1.37 us

profile of v5, /device:TPU:1, one launch (start us, length us, event | category | flops | bytes accessed | tf_op | source)
XLA Modules:
  0.0 52.4 jit_solution(7307917175279316248)
XLA Ops:
  0.6 50.4 %shard_map.86 = (f32[32,256]{1,0:T(8,128)S(1)}, f32[32,16384]{1,0:T(8,128)S(1)}) custom-call(bf16[16384,256]{1,0:T(8,128)(2,1)} %design.1, bf16[32,256]{1,0:T(8,128)(2,1)} %bitcast.11, f32[1,32]{1,0:T(1,128)} %bitcast.12, f32[128,128]{1,0:T(8,128)} %bitcast.7, s32[128,128]{1,0:T(8,128)} %bitcast.8, s32[128,128]{1,0:T(8,128)} %bitcast.9, s32[128,128]{1,0:T(8,128)} %bitcast.10), custom_call_target="tpu_custom_call" | custom-call | flops 536870912 | bytes 10485760 | tf_op jit(solution)/shard_map/pallas_call | solution.py:423
  51.1 1.4 %shard_map.87 = (f32[32,256]{1,0:T(8,128)}, f32[32,16384]{1,0:T(8,128)}) custom-call(f32[32,256]{1,0:T(8,128)S(1)} %get-tuple-element.6.new, f32[32,16384]{1,0:T(8,128)S(1)} %get-tuple-element.7.weights), custom_call_target="tpu_custom_call" | custom-call | tf_op jit(solution)/shard_map/pallas_call | solution.py:480

commit v6 on v5

--- a/solution.py
+++ b/solution.py
@@ -22,6 +22,7 @@
 EIGHTH = BLOCKS // 8
 CHUNK = ROWS // 4
 NBATCH = 2
+AHEAD = 3
 CHUNKS = ((0, 0, 16), (1, 0, 16), (0, 16, 16), (1, 16, 16), (0, 32, 16), (1, 32, 16), (0, 48, 16), (1, 48, 16))
 FAR_FIRST = (4, 3, 5, 2, 6, 1, 7)
 
@@ -72,7 +73,7 @@
 def kernel(
     design, coefs, penalty, censor, codes, first, last,
     new_out, weights_out,
-    D, C, PEN, CEN, COD, FST, LST, IC2, E, R1, R2, S, R4, ETA, EX, BASE, TS, TR, W, SP, SR, SUM,
+    D, C, PEN, CEN, COD, FST, LST, IC2, E, R1, R2, S, R4, ETA, EX, INV, BASE, TS, TR, W, SP, SR, SUM,
     load_sem, send_sem, recv_sem,
 ):
     s = lax.axis_index("subj")
@@ -133,9 +134,7 @@
     ):
         small.append(pltpu.make_async_copy(src, dst, load_sem.at[len(CHUNKS) + i]))
     small[0].start()
-    for copy in chunks:
-        copy.start()
-    for copy in small[1:]:
+    for copy in chunks[:AHEAD]:
         copy.start()
 
     small[0].wait()
@@ -232,13 +231,15 @@
 
     def scan_a(k):
         expo = jnp.exp(ETA[k])
-        comp = expo * IC2[...]
         EX[k] = expo
         TS[k, 0, 0] = fold(expo)
-        TS[k, 0, 1] = fold(comp)
+        TS[k, 0, 1] = fold(expo * IC2[...])
         exchange(k, 0)
+
+    def scan_a_local(k):
+        expo = EX[k]
         risk, risk_rows = lane_scan(expo, "ge")
-        before, before_rows = lane_scan(comp, "lt")
+        before, before_rows = lane_scan(expo * IC2[...], "lt")
         lanes = FST[...]
         BASE[k] = (pick(risk, lanes) + row_scan(risk_rows, "lt")) + CEN[...] * (
             pick(before, lanes) + row_scan(before_rows, "gt")
@@ -248,12 +249,15 @@
         risk_in, comp_in = arrived(k, 0)
         risk = BASE[k] + (risk_in + CEN[...] * comp_in)
         inv = jnp.where(COD[...] == 1, 1.0 / risk, 0.0)
-        heavy = inv * CEN[...]
-        TS[k, 1, 0] = fold(heavy)
+        INV[k] = inv
+        TS[k, 1, 0] = fold(inv * CEN[...])
         TS[k, 1, 1] = fold(inv)
         exchange(k, 1)
+
+    def scan_b_local(k):
+        inv = INV[k]
         upto, upto_rows = lane_scan(inv, "le")
-        later, later_rows = lane_scan(heavy, "gt")
+        later, later_rows = lane_scan(inv * CEN[...], "gt")
         lanes = LST[...]
         BASE[k] = (pick(upto, lanes) + row_scan(upto_rows, "gt")) + IC2[...] * (
             pick(later, lanes) + row_scan(later_rows, "lt")
@@ -313,6 +317,11 @@
     both = (0, 1)
     for i, (h, first_block, blocks) in enumerate(CHUNKS):
         chunks[i].wait()
+        if i + AHEAD < len(chunks):
+            chunks[i + AHEAD].start()
+        elif i + AHEAD == len(chunks):
+            for copy in small[1:]:
+                copy.start()
         predict(h, first_block, blocks)
         if i == 0:
             pl.semaphore_wait(barrier, len(peers))
@@ -344,14 +353,16 @@
         rs_second(h, 1, 0)
     for h in both:
         rs_second(h, 1, 1)
-    for h in both:
-        rs_end(h, 0)
-    scan_a(0)
-    for h in both:
-        rs_end(h, 1)
-    scan_a(1)
+    for k in both:
+        for h in both:
+            rs_end(h, k)
+        scan_a(k)
+    for k in both:
+        scan_a_local(k)
     for k in both:
         scan_b(k)
+    for k in both:
+        scan_b_local(k)
     for k in both:
         scan_c(k)
         for part in both:
@@ -442,6 +453,7 @@
             vmem((2, NBATCH, 2, RING, HALF, LANES), F32),
             vmem((2, NBATCH, RING, HALF, LANES), F32),
             vmem((2, NBATCH, 3, HALF, LANES), F32),
+            vmem((NBATCH, BLOCKS, LANES), F32),
             vmem((NBATCH, BLOCKS, LANES), F32),
             vmem((NBATCH, BLOCKS, LANES), F32),
             vmem((NBATCH, BLOCKS, LANES), F32),

time: 52.6 us -> 52.5 us (level)
  no operation moved by 1% of the time
where the time goes in v6:
time: 52.5 us; the launch traced here: 52.3 us
  Pallas kernels  51.7 us (98%)
  between operations  0.64 us (1%)
    pallas_call x1, Pallas kernels, local(): pl.pallas_call(kernel, out_shape=(jax.ShapeDtypeStruct((PATHS, COLS), F32...  50.3 us
    pallas_call x1, Pallas kernels, local(): pl.pallas_call(hand_over, out_shape=(jax.ShapeDtypeStruct((PATHS, COLS),...  1.37 us

profile of v6, /device:TPU:1, one launch (start us, length us, event | category | flops | bytes accessed | tf_op | source)
XLA Modules:
  0.0 52.3 jit_solution(10062665358292630074)
XLA Ops:
  0.6 50.3 %shard_map.86 = (f32[32,256]{1,0:T(8,128)S(1)}, f32[32,16384]{1,0:T(8,128)S(1)}) custom-call(bf16[16384,256]{1,0:T(8,128)(2,1)} %design.1, bf16[32,256]{1,0:T(8,128)(2,1)} %bitcast.11, f32[1,32]{1,0:T(1,128)} %bitcast.12, f32[128,128]{1,0:T(8,128)} %bitcast.7, s32[128,128]{1,0:T(8,128)} %bitcast.8, s32[128,128]{1,0:T(8,128)} %bitcast.9, s32[128,128]{1,0:T(8,128)} %bitcast.10), custom_call_target="tpu_custom_call" | custom-call | flops 536870912 | bytes 10485760 | tf_op jit(solution)/shard_map/pallas_call | solution.py:434
  51.0 1.4 %shard_map.87 = (f32[32,256]{1,0:T(8,128)}, f32[32,16384]{1,0:T(8,128)}) custom-call(f32[32,256]{1,0:T(8,128)S(1)} %get-tuple-element.6.new, f32[32,16384]{1,0:T(8,128)S(1)} %get-tuple-element.7.weights), custom_call_target="tpu_custom_call" | custom-call | tf_op jit(solution)/shard_map/pallas_call | solution.py:492

commit v7 on v6

--- a/solution.py
+++ b/solution.py
@@ -82,8 +82,8 @@
     z = cov % RING
     pos = (x, z)
 
-    E5 = E.reshape(RING, RING, 2, BLOCKS, LANES)
-    W5 = W.reshape(RING, RING, 2, BLOCKS, LANES)
+    E5 = E.at[pl.ds(0, PATHS * BLOCKS)].reshape(RING, RING, 2, BLOCKS, LANES)
+    W5 = W.at[pl.ds(0, PATHS * BLOCKS)].reshape(RING, RING, 2, BLOCKS, LANES)
 
     def device(axis, at):
         return (s, at * RING + z) if axis == 0 else (s, x * RING + at)
@@ -340,19 +340,19 @@
     for h in both:
         for d in both:
             rs_near(h, 1, 1, d)
+    for h in both:
+        rs_on(h, 1, 0)
+    for h in both:
+        rs_second(h, 0, 0)
+    for h in both:
+        rs_on(h, 1, 1)
+    for h in both:
+        rs_second(h, 0, 1)
+    for h in both:
+        rs_second(h, 1, 0)
+    for h in both:
+        rs_second(h, 1, 1)
     prepare()
-    for h in both:
-        rs_on(h, 1, 0)
-    for h in both:
-        rs_second(h, 0, 0)
-    for h in both:
-        rs_on(h, 1, 1)
-    for h in both:
-        rs_second(h, 0, 1)
-    for h in both:
-        rs_second(h, 1, 0)
-    for h in both:
-        rs_second(h, 1, 1)
     for k in both:
         for h in both:
             rs_end(h, k)
@@ -408,7 +408,7 @@
     scale = 0.1 / jnp.sqrt(F32(SUBJ * ROWS))
     for c in range(2):
         cols = slice(c * LANES, (c + 1) * LANES)
-        shifted = wide[:, cols] + scale * SUM[c]
+        shifted = wide[:, cols] + scale * SUM[c, 0:PATHS, :]
         sign = jnp.where(shifted > 0, 1.0, jnp.where(shifted < 0, -1.0, 0.0))
         new_out[:, cols] = sign * jnp.maximum(jnp.abs(shifted) - limit, 0.0)
     left_rows = sent_rows[0]
@@ -448,7 +448,7 @@
             vmem(square, jnp.int32),
             vmem(square, jnp.int32),
             vmem(square, F32),
-            vmem((PATHS * BLOCKS, LANES), F32),
+            vmem((PATHS * BLOCKS + BLOCKS, LANES), F32),
             vmem((2, NBATCH, 2, 2, RING, EIGHTH, LANES), F32),
             vmem((2, NBATCH, 2, RING, HALF, LANES), F32),
             vmem((2, NBATCH, RING, HALF, LANES), F32),
@@ -459,10 +459,10 @@
             vmem((NBATCH, BLOCKS, LANES), F32),
             vmem((NBATCH, 2, 2, 8, LANES), F32),
             vmem((NBATCH, 2, SUBJ, 2, 8, LANES), F32),
-            vmem((PATHS * BLOCKS, LANES), F32),
+            vmem((PATHS * BLOCKS + 2 * BLOCKS, LANES), F32),
             vmem((NBATCH, PATHS // 2, COLS), F32),
             vmem((NBATCH, SUBJ, PATHS // 2, COLS), F32),
-            vmem((2, PATHS, LANES), F32),
+            vmem((2, PATHS + 8, LANES), F32),
             dma((len(CHUNKS) + 6,)),
             dma((1,)),
             dma((50,)),

time: 52.5 us -> 52.5 us (level)
  no operation moved by 1% of the time
where the time goes in v7:
time: 52.5 us; the launch traced here: 52.3 us
  Pallas kernels  51.7 us (98%)
  between operations  0.64 us (1%)
    pallas_call x1, Pallas kernels, local(): pl.pallas_call(kernel, out_shape=(jax.ShapeDtypeStruct((PATHS, COLS), F32...  50.3 us
    pallas_call x1, Pallas kernels, local(): pl.pallas_call(hand_over, out_shape=(jax.ShapeDtypeStruct((PATHS, COLS),...  1.37 us

profile of v7, /device:TPU:1, one launch (start us, length us, event | category | flops | bytes accessed | tf_op | source)
XLA Modules:
  0.0 52.3 jit_solution(3709512387796903267)
XLA Ops:
  0.6 50.3 %shard_map.86 = (f32[32,256]{1,0:T(8,128)S(1)}, f32[32,16384]{1,0:T(8,128)S(1)}) custom-call(bf16[16384,256]{1,0:T(8,128)(2,1)} %design.1, bf16[32,256]{1,0:T(8,128)(2,1)} %bitcast.11, f32[1,32]{1,0:T(1,128)} %bitcast.12, f32[128,128]{1,0:T(8,128)} %bitcast.7, s32[128,128]{1,0:T(8,128)} %bitcast.8, s32[128,128]{1,0:T(8,128)} %bitcast.9, s32[128,128]{1,0:T(8,128)} %bitcast.10), custom_call_target="tpu_custom_call" | custom-call | flops 536870912 | bytes 10485760 | tf_op jit(solution)/shard_map/pallas_call | solution.py:434
  51.0 1.4 %shard_map.87 = (f32[32,256]{1,0:T(8,128)}, f32[32,16384]{1,0:T(8,128)}) custom-call(f32[32,256]{1,0:T(8,128)S(1)} %get-tuple-element.6.new, f32[32,16384]{1,0:T(8,128)S(1)} %get-tuple-element.7.weights), custom_call_target="tpu_custom_call" | custom-call | tf_op jit(solution)/shard_map/pallas_call | solution.py:492

commit v8 on v7

--- a/solution.py
+++ b/solution.py
@@ -22,7 +22,7 @@
 EIGHTH = BLOCKS // 8
 CHUNK = ROWS // 4
 NBATCH = 2
-AHEAD = 3
+AHEAD = 4
 CHUNKS = ((0, 0, 16), (1, 0, 16), (0, 16, 16), (1, 16, 16), (0, 32, 16), (1, 32, 16), (0, 48, 16), (1, 48, 16))
 FAR_FIRST = (4, 3, 5, 2, 6, 1, 7)
 

time: 52.5 us -> 52.5 us (level)
  no operation moved by 1% of the time
where the time goes in v8:
time: 52.5 us; the launch traced here: 52.3 us
  Pallas kernels  51.7 us (98%)
  between operations  0.64 us (1%)
    pallas_call x1, Pallas kernels, local(): pl.pallas_call(kernel, out_shape=(jax.ShapeDtypeStruct((PATHS, COLS), F32...  50.3 us
    pallas_call x1, Pallas kernels, local(): pl.pallas_call(hand_over, out_shape=(jax.ShapeDtypeStruct((PATHS, COLS),...  1.37 us

profile of v8, /device:TPU:1, one launch (start us, length us, event | category | flops | bytes accessed | tf_op | source)
XLA Modules:
  0.0 52.3 jit_solution(17176755120196102078)
XLA Ops:
  0.6 50.3 %shard_map.86 = (f32[32,256]{1,0:T(8,128)S(1)}, f32[32,16384]{1,0:T(8,128)S(1)}) custom-call(bf16[16384,256]{1,0:T(8,128)(2,1)} %design.1, bf16[32,256]{1,0:T(8,128)(2,1)} %bitcast.11, f32[1,32]{1,0:T(1,128)} %bitcast.12, f32[128,128]{1,0:T(8,128)} %bitcast.7, s32[128,128]{1,0:T(8,128)} %bitcast.8, s32[128,128]{1,0:T(8,128)} %bitcast.9, s32[128,128]{1,0:T(8,128)} %bitcast.10), custom_call_target="tpu_custom_call" | custom-call | flops 536870912 | bytes 10485760 | tf_op jit(solution)/shard_map/pallas_call | solution.py:434
  51.0 1.4 %shard_map.87 = (f32[32,256]{1,0:T(8,128)}, f32[32,16384]{1,0:T(8,128)}) custom-call(f32[32,256]{1,0:T(8,128)S(1)} %get-tuple-element.6.new, f32[32,16384]{1,0:T(8,128)S(1)} %get-tuple-element.7.weights), custom_call_target="tpu_custom_call" | custom-call | tf_op jit(solution)/shard_map/pallas_call | solution.py:492
